TPU v7x, 256 devices: a whole 4x4x8 slice. The times are simulated.
256 devices in a mesh: row: 8 (over x, z_hi), col: 32 (over z_lo, y, core).
Axes of the slice: x: 4, y: 4, z: 8 (z_hi: 2, z_lo: 4; z = z_hi * 4 + z_lo), core: 2. Of those that a mesh axis runs over, the one named last changes fastest.
Arguments:
- pair_map: bfloat16 [32, 1024, 1024], P(None, 'col', 'row'), may hold values from -6 to 6
- out_grad: bfloat16 [32, 1024, 1024], P(None, 'col', 'row'), may hold values from -6 to 6
- first_a: bfloat16 [3, 3, 32, 32], replicated, may hold values from -0.375 to 0.375
- first_b: bfloat16 [3, 3, 32, 32], replicated, may hold values from -0.375 to 0.375
- second_a: bfloat16 [3, 3, 32, 32], replicated, may hold values from -0.375 to 0.375
- second_b: bfloat16 [3, 3, 32, 32], replicated, may hold values from -0.375 to 0.375
Outputs:
- decoded: bfloat16 [32, 1024, 1024], P(None, 'col', 'row')
- grad_map: bfloat16 [32, 1024, 1024], P(None, 'col', 'row')
- grad_first_a: float32 [3, 3, 32, 32], replicated
- grad_first_b: float32 [3, 3, 32, 32], replicated
- grad_second_a: float32 [3, 3, 32, 32], replicated
- grad_second_b: float32 [3, 3, 32, 32], replicated
All inputs are finite; a program needn't handle non-finite values.
Results may differ from a plain program's by a relative error of at most 0.0078.
Values may be sent and summed in bfloat16 or wider, within the bound.
A program may use at most 128 MiB of HBM per device.

v0:
```python
import jax
import jax.numpy as jnp
from jax import lax
from jax.sharding import PartitionSpec as P

DILATE_ONE = 4
DILATE_TWO = 8


def padded_2(block, sides, width):
    for axis, dim in sides:
        count = lax.axis_size(axis)
        forward = [(i, i + 1) for i in range(count - 1)]
        backward = [(target, source) for source, target in forward]
        low = lax.ppermute(
            lax.slice_in_dim(block, block.shape[dim] - width, None, axis=dim), axis, forward
        )
        high = lax.ppermute(lax.slice_in_dim(block, 0, width, axis=dim), axis, backward)
        block = jnp.concatenate([low, block, high], axis=dim)
    return block


def widen(field, spacing):
    return padded_2(field, (("row", 2), ("col", 1)), spacing)


def apply_taps(padded, kernel, spacing, height, breadth):
    total = jnp.zeros((kernel.shape[2], height, breadth), jnp.float32)
    for row_tap in range(3):
        for col_tap in range(3):
            shifted = padded[
                :,
                row_tap * spacing : row_tap * spacing + height,
                col_tap * spacing : col_tap * spacing + breadth,
            ]
            total = total + jnp.einsum(
                "oi,irc->orc", kernel[row_tap, col_tap], shifted, preferred_element_type=jnp.float32
            )
    return total


def local_kernel_grad(padded, cotangent, spacing):
    height = cotangent.shape[1]
    breadth = cotangent.shape[2]
    outer = []
    for row_tap in range(3):
        inner = []
        for col_tap in range(3):
            shifted = padded[
                :,
                row_tap * spacing : row_tap * spacing + height,
                col_tap * spacing : col_tap * spacing + breadth,
            ]
            inner.append(
                jnp.einsum("orc,irc->oi", cotangent, shifted, preferred_element_type=jnp.float32)
            )
        outer.append(jnp.stack(inner))
    return jnp.stack(outer)


def flipped(kernel):
    return jnp.swapaxes(kernel[::-1, ::-1], 2, 3)


def mirror(field):
    spread = lax.all_to_all(field, "row", split_axis=0, concat_axis=2, tiled=True)
    turned = lax.all_to_all(spread, "col", split_axis=2, concat_axis=1, tiled=True)
    gathered = lax.all_to_all(turned, "row", split_axis=1, concat_axis=0, tiled=True)
    return jnp.swapaxes(gathered, 1, 2)


def averaged_with_mirror(field):
    return ((field.astype(jnp.float32) + mirror(field).astype(jnp.float32)) * 0.5).astype(
        jnp.bfloat16
    )


def silu_slope(before):
    sigmoid_value = jax.nn.sigmoid(before)
    return sigmoid_value * (1.0 + before * (1.0 - sigmoid_value))


def per_device(pair_map, out_grad, first_a, first_b, second_a, second_b):
    height = pair_map.shape[1]
    breadth = pair_map.shape[2]
    spacings = (DILATE_ONE, DILATE_TWO)
    kernels = ((first_a, first_b), (second_a, second_b))
    current = pair_map
    stored = []
    for block_index in range(2):
        kernel_a, kernel_b = kernels[block_index]
        spacing = spacings[block_index]
        padded_source = widen(current, spacing)
        before = apply_taps(padded_source, kernel_a, spacing, height, breadth)
        hidden = jax.nn.silu(before).astype(jnp.bfloat16)
        padded_hidden = widen(hidden, spacing)
        summed = (
            current.astype(jnp.float32)
            + apply_taps(padded_hidden, kernel_b, spacing, height, breadth)
        ).astype(jnp.bfloat16)
        stored.append((padded_source, before, padded_hidden))
        current = averaged_with_mirror(summed)
    upstream = out_grad
    kernel_grads = [None, None, None, None]
    for block_index in (1, 0):
        kernel_a, kernel_b = kernels[block_index]
        spacing = spacings[block_index]
        padded_source, before, padded_hidden = stored[block_index]
        averaged = averaged_with_mirror(upstream)
        kernel_grads[2 * block_index + 1] = local_kernel_grad(padded_hidden, averaged, spacing)
        padded_averaged = widen(averaged, spacing)
        hidden_grad = apply_taps(padded_averaged, flipped(kernel_b), spacing, height, breadth)
        inner_grad = (hidden_grad * silu_slope(before)).astype(jnp.bfloat16)
        kernel_grads[2 * block_index] = local_kernel_grad(padded_source, inner_grad, spacing)
        padded_inner = widen(inner_grad, spacing)
        upstream = (
            averaged.astype(jnp.float32)
            + apply_taps(padded_inner, flipped(kernel_a), spacing, height, breadth)
        ).astype(jnp.bfloat16)
    totals = lax.psum(
        (kernel_grads[0], kernel_grads[1], kernel_grads[2], kernel_grads[3]), ("row", "col")
    )
    return (current, upstream, totals[0], totals[1], totals[2], totals[3])


def solution(mesh):
    return jax.shard_map(
        per_device,
        mesh=mesh,
        in_specs=(P(None, "col", "row"), P(None, "col", "row"), P(), P(), P(), P()),
        out_specs=(P(None, "col", "row"), P(None, "col", "row"), P(), P(), P(), P()),
        check_vma=False,
    )
```

profile of v0, /device:TPU:1, one launch (start us, length us, event | category | flops | bytes accessed | tf_op | source)
XLA Modules:
  0.0 763.8 jit_solution(13582284896597658730)
XLA Ops:
  7.2 11.6 %all-to-all-start.6 = ((bf16[32,32,128]{2,1,0:T(8,128)(2,1)}), bf16[32,32,128]{2,1,0:T(8,128)(2,1)}, u32[]{:S(2)}, u32[]{:S(2)}) async-start(bf16[32,32,128]{2,1,0:T(8,128)(2,1)} %param.7), calls=%async_computation.6 | async-start | bytes 524288 | tf_op jit(solution)/shard_map/all_to_all | solution.py:66
  21.3 7.9 %collective-permute-start = (bf16[32,32,4]{2,0,1:T(8,128)(2,1)S(1)}, bf16[32,32,4]{2,0,1:T(8,128)(2,1)S(1)}, u32[]{:S(2)}, u32[]{:S(2)}) collective-permute-start(bf16[32,32,4]{2,0,1:T(8,128)(2,1)S(1)} %get-tuple-element.81), channel_id=1, source_target_pairs={{0,32},{32,64},{64,96},{96,128},{128,160},{160,192},{192,224},{1,3... | collective-permute-start | bytes 24584 | tf_op jit(solution)/shard_map/ppermute | solution.py:15
  29.5 7.4 collective-permute-done.1
  47.4 12.2 %collective-permute-start.4 = (bf16[32,32,4]{2,0,1:T(8,128)(2,1)S(1)}, bf16[32,32,4]{2,0,1:T(8,128)(2,1)S(1)}, u32[]{:S(2)}, u32[]{:S(2)}) collective-permute-start(bf16[32,32,4]{2,0,1:T(8,128)(2,1)S(1)} %get-tuple-element.78), channel_id=1, source_target_pairs={{0,32},{32,64},{64,96},{96,128},{128,160},{160,192},{192,224},{1,3... | collective-permute-start | bytes 24584 | tf_op jit(solution)/shard_map/ppermute | solution.py:15
  61.1 3.9 collective-permute-done.4
  65.0 21.8 %collective-permute-done.5 = bf16[32,32,4]{2,0,1:T(8,128)(2,1)S(1)} collective-permute-done((bf16[32,32,4]{2,0,1:T(8,128)(2,1)S(1)}, bf16[32,32,4]{2,0,1:T(8,128)(2,1)S(1)}, u32[]{:S(2)}, u32[]{:S(2)}) %collective-permute-start.5) | collective-permute-done | bytes 8224 | tf_op jit(solution)/shard_map/ppermute | solution.py:18
  87.0 4.4 collective-permute-start.6
  93.7 3.4 collective-permute-done.7
  100.4 14.0 %all-to-all-start = ((bf16[32,32,128]{2,1,0:T(8,128)(2,1)}), bf16[32,32,128]{2,1,0:T(8,128)(2,1)S(1)}, u32[]{:S(2)}, u32[]{:S(2)}) async-start(bf16[32,32,128]{2,1,0:T(8,128)(2,1)} %copy.103), calls=%async_computation | async-start | bytes 524288 | tf_op jit(solution)/shard_map/all_to_all | solution.py:66
  117.6 7.5 all-to-all-done
  125.1 8.3 %all-to-all-start.7 = ((bf16[32,2,2048]{2,1,0:T(2,128)(2,1)}), bf16[32,2,2048]{2,1,0:T(2,128)(2,1)S(1)}, u32[]{:S(2)}, u32[]{:S(2)}) async-start(bf16[32,2,2048]{2,1,0:T(2,128)(2,1)} %reshape.152), calls=%async_computation.7 | async-start | bytes 524288 | tf_op jit(solution)/shard_map/all_to_all | solution.py:67
  135.9 8.7 %all-to-all-done.7 = bf16[32,2,2048]{2,1,0:T(2,128)(2,1)S(1)} async-done(((bf16[32,2,2048]{2,1,0:T(2,128)(2,1)}), bf16[32,2,2048]{2,1,0:T(2,128)(2,1)S(1)}, u32[]{:S(2)}, u32[]{:S(2)}) %all-to-all-start.7) | async-done | bytes 262176 | tf_op jit(solution)/shard_map/all_to_all | solution.py:67
  144.6 4.1 all-to-all-start.1
  152.8 6.9 all-to-all-done.1
  159.7 4.0 all-to-all-start.8
  170.9 4.1 all-to-all-done.8
  175.1 4.8 all-to-all-start.2
  184.0 7.3 collective-permute-start.16
  192.8 3.6 collective-permute-done.16
  196.4 12.3 %collective-permute-done.17 = bf16[32,32,8]{2,0,1:T(8,128)(2,1)S(1)} collective-permute-done((bf16[32,32,8]{2,0,1:T(8,128)(2,1)S(1)}, bf16[32,32,8]{2,0,1:T(8,128)(2,1)S(1)}, u32[]{:S(2)}, u32[]{:S(2)}) %collective-permute-start.17) | collective-permute-done | bytes 16416 | tf_op jit(solution)/shard_map/ppermute | solution.py:18
  209.6 4.6 collective-permute-start.18
  221.1 11.2 %collective-permute-start.8 = (bf16[32,32,8]{2,0,1:T(8,128)(2,1)S(1)}, bf16[32,32,8]{2,0,1:T(8,128)(2,1)S(1)}, u32[]{:S(2)}, u32[]{:S(2)}) collective-permute-start(bf16[32,32,8]{2,0,1:T(8,128)(2,1)S(1)} %get-tuple-element.76), channel_id=1, source_target_pairs={{0,32},{32,64},{64,96},{96,128},{128,160},{160,192},{192,224},{1,3... | collective-permute-start | bytes 49160 | tf_op jit(solution)/shard_map/ppermute | solution.py:15
  237.1 11.5 %collective-permute-done.9 = bf16[32,32,8]{2,0,1:T(8,128)(2,1)S(1)} collective-permute-done((bf16[32,32,8]{2,0,1:T(8,128)(2,1)S(1)}, bf16[32,32,8]{2,0,1:T(8,128)(2,1)S(1)}, u32[]{:S(2)}, u32[]{:S(2)}) %collective-permute-start.9) | collective-permute-done | bytes 16416 | tf_op jit(solution)/shard_map/ppermute | solution.py:18
  248.8 3.9 collective-permute-start.10
  254.9 4.1 collective-permute-done.11
  266.1 9.5 %collective-permute-start.20 = (bf16[32,32,8]{2,0,1:T(8,128)(2,1)S(1)}, bf16[32,32,8]{2,0,1:T(8,128)(2,1)S(1)}, u32[]{:S(2)}, u32[]{:S(2)}) collective-permute-start(bf16[32,32,8]{2,0,1:T(8,128)(2,1)S(1)} %get-tuple-element.70), channel_id=1, source_target_pairs={{0,32},{32,64},{64,96},{96,128},{128,160},{160,192},{192,224},{1,3... | collective-permute-start | bytes 49160 | tf_op jit(solution)/shard_map/ppermute | solution.py:15
  276.9 7.9 %collective-permute-start.12 = (bf16[32,32,8]{2,0,1:T(8,128)(2,1)S(1)}, bf16[32,32,8]{2,0,1:T(8,128)(2,1)S(1)}, u32[]{:S(2)}, u32[]{:S(2)}) collective-permute-start(bf16[32,32,8]{2,0,1:T(8,128)(2,1)S(1)} %get-tuple-element.74), channel_id=1, source_target_pairs={{0,32},{32,64},{64,96},{96,128},{128,160},{160,192},{192,224},{1,3... | collective-permute-start | bytes 49160 | tf_op jit(solution)/shard_map/ppermute | solution.py:15
  287.5 13.2 %collective-permute-done.21 = bf16[32,32,8]{2,0,1:T(8,128)(2,1)S(1)} collective-permute-done((bf16[32,32,8]{2,0,1:T(8,128)(2,1)S(1)}, bf16[32,32,8]{2,0,1:T(8,128)(2,1)S(1)}, u32[]{:S(2)}, u32[]{:S(2)}) %collective-permute-start.21) | collective-permute-done | bytes 16416 | tf_op jit(solution)/shard_map/ppermute | solution.py:18
  306.1 3.8 collective-permute-done.13
  310.2 5.3 collective-permute-start.14
  330.6 17.2 %all-to-all-start.9 = ((bf16[32,32,128]{2,1,0:T(8,128)(2,1)}), bf16[32,32,128]{2,1,0:T(8,128)(2,1)}, u32[]{:S(2)}, u32[]{:S(2)}) async-start(bf16[32,32,128]{2,1,0:T(8,128)(2,1)} %copy.126), calls=%async_computation.9 | async-start | bytes 524288 | tf_op jit(solution)/shard_map/all_to_all | solution.py:66
  352.6 5.5 all-to-all-done.9
  358.0 4.1 all-to-all-start.3
  366.0 6.5 all-to-all-done.3
  372.5 11.5 %all-to-all-start.10 = ((bf16[32,2,2048]{2,1,0:T(2,128)(2,1)}), bf16[32,2,2048]{2,1,0:T(2,128)(2,1)}, u32[]{:S(2)}, u32[]{:S(2)}) async-start(bf16[32,2,2048]{2,1,0:T(2,128)(2,1)} %reshape.156), calls=%async_computation.10 | async-start | bytes 524288 | tf_op jit(solution)/shard_map/all_to_all | solution.py:67
  387.8 7.4 all-to-all-done.10
  395.1 4.4 all-to-all-start.4
  406.3 4.6 all-to-all-done.4
  410.8 3.6 all-to-all-start.11
  425.6 5.8 all-to-all-start.5
  435.8 5.9 all-to-all-done.5
  453.4 12.9 %collective-permute-done.25 = bf16[32,32,4]{2,0,1:T(8,128)(2,1)S(1)} collective-permute-done((bf16[32,32,4]{2,0,1:T(8,128)(2,1)S(1)}, bf16[32,32,4]{2,0,1:T(8,128)(2,1)S(1)}, u32[]{:S(2)}, u32[]{:S(2)}) %collective-permute-start.25) | collective-permute-done | bytes 8224 | tf_op jit(solution)/shard_map/ppermute | solution.py:18
  466.4 4.0 collective-permute-start.26
  482.4 10.6 %collective-permute-start.28 = (bf16[32,32,4]{2,0,1:T(8,128)(2,1)S(1)}, bf16[32,32,4]{2,0,1:T(8,128)(2,1)S(1)}, u32[]{:S(2)}, u32[]{:S(2)}) collective-permute-start(bf16[32,32,4]{2,0,1:T(8,128)(2,1)S(1)} %get-tuple-element.66), channel_id=1, source_target_pairs={{0,32},{32,64},{64,96},{96,128},{128,160},{160,192},{192,224},{1,3... | collective-permute-start | bytes 24584 | tf_op jit(solution)/shard_map/ppermute | solution.py:15
  495.7 7.8 %collective-permute-done.28 = bf16[32,32,4]{2,0,1:T(8,128)(2,1)S(1)} collective-permute-done((bf16[32,32,4]{2,0,1:T(8,128)(2,1)S(1)}, bf16[32,32,4]{2,0,1:T(8,128)(2,1)S(1)}, u32[]{:S(2)}, u32[]{:S(2)}) %collective-permute-start.28) | collective-permute-done | bytes 8224 | tf_op jit(solution)/shard_map/ppermute | solution.py:15
  503.5 8.0 %collective-permute-done.29 = bf16[32,32,4]{2,0,1:T(8,128)(2,1)S(1)} collective-permute-done((bf16[32,32,4]{2,0,1:T(8,128)(2,1)S(1)}, bf16[32,32,4]{2,0,1:T(8,128)(2,1)S(1)}, u32[]{:S(2)}, u32[]{:S(2)}) %collective-permute-start.29) | collective-permute-done | bytes 8224 | tf_op jit(solution)/shard_map/ppermute | solution.py:18
  516.3 3.7 collective-permute-done.31
  523.3 227.1 %all-reduce.3.cloned.1.call-done = (f32[3,3,32,32]{3,2,1,0:T(8,128)}, f32[3,3,32,32]{3,2,1,0:T(8,128)}, f32[3,3,32,32]{3,2,1,0:T(8,128)}, f32[3,3,32,32]{3,2,1,0:T(8,128)}) async-done(((f32[3,3,32,32]{3,2,1,0:T(8,128)}, f32[3,3,32,32]{3,2,1,0:T(8,128)}, f32[3,3,32,32]{3,2,1,0:T(8,128)}, f32[3,3,32,32]{3,2,1,0:T(8,128)}), (f32[3,3,32,32]{3,2,1,0:T(8,128)}, f32[3,3,32,32]{3,2,1,0:T(8,128)}, ...) | async-done | bytes 147472 | tf_op jit(solution)/shard_map/psum | solution.py:120
  (331 shorter events, 164.0 us)
Async XLA Ops:
  7.2 22.1 %copy-start.15 = (bf16[32,32,128]{2,1,0:T(8,128)(2,1)S(1)}, bf16[32,32,128]{2,1,0:T(8,128)(2,1)}, u32[]{:S(2)}) copy-start(bf16[32,32,128]{2,1,0:T(8,128)(2,1)} %param.6) | copy-start | bytes 786436
  7.2 93.2 %all-to-all-start.6 = ((bf16[32,32,128]{2,1,0:T(8,128)(2,1)}), bf16[32,32,128]{2,1,0:T(8,128)(2,1)}, u32[]{:S(2)}, u32[]{:S(2)}) async-start(bf16[32,32,128]{2,1,0:T(8,128)(2,1)} %param.7), calls=%async_computation.6 | async-start | bytes 524288 | tf_op jit(solution)/shard_map/all_to_all | solution.py:66
  20.0 16.9 %collective-permute-start.1 = (bf16[32,32,4]{2,0,1:T(8,128)(2,1)S(1)}, bf16[32,32,4]{2,0,1:T(8,128)(2,1)S(1)}, u32[]{:S(2)}, u32[]{:S(2)}) collective-permute-start(bf16[32,32,4]{2,0,1:T(8,128)(2,1)S(1)} %get-tuple-element.80), channel_id=1, source_target_pairs={{32,0},{64,32},{96,64},{128,96},{160,128},{192,160},{224,192},{33,... | collective-permute-start | bytes 24584 | tf_op jit(solution)/shard_map/ppermute | solution.py:18
  21.3 15.6 %collective-permute-start = (bf16[32,32,4]{2,0,1:T(8,128)(2,1)S(1)}, bf16[32,32,4]{2,0,1:T(8,128)(2,1)S(1)}, u32[]{:S(2)}, u32[]{:S(2)}) collective-permute-start(bf16[32,32,4]{2,0,1:T(8,128)(2,1)S(1)} %get-tuple-element.81), channel_id=1, source_target_pairs={{0,32},{32,64},{64,96},{96,128},{128,160},{160,192},{192,224},{1,3... | collective-permute-start | bytes 24584 | tf_op jit(solution)/shard_map/ppermute | solution.py:15
  37.0 5.9 collective-permute-start.3
  39.5 4.4 collective-permute-start.2
  47.4 17.6 %collective-permute-start.4 = (bf16[32,32,4]{2,0,1:T(8,128)(2,1)S(1)}, bf16[32,32,4]{2,0,1:T(8,128)(2,1)S(1)}, u32[]{:S(2)}, u32[]{:S(2)}) collective-permute-start(bf16[32,32,4]{2,0,1:T(8,128)(2,1)S(1)} %get-tuple-element.78), channel_id=1, source_target_pairs={{0,32},{32,64},{64,96},{96,128},{128,160},{160,192},{192,224},{1,3... | collective-permute-start | bytes 24584 | tf_op jit(solution)/shard_map/ppermute | solution.py:15
  59.6 27.3 %collective-permute-start.5 = (bf16[32,32,4]{2,0,1:T(8,128)(2,1)S(1)}, bf16[32,32,4]{2,0,1:T(8,128)(2,1)S(1)}, u32[]{:S(2)}, u32[]{:S(2)}) collective-permute-start(bf16[32,32,4]{2,0,1:T(8,128)(2,1)S(1)} %get-tuple-element.79), channel_id=1, source_target_pairs={{32,0},{64,32},{96,64},{128,96},{160,128},{192,160},{224,192},{33,... | collective-permute-start | bytes 24584 | tf_op jit(solution)/shard_map/ppermute | solution.py:18
  65.0 32.5 %copy-start.6 = (bf16[32,32,4]{2,0,1:T(8,128)(2,1)}, bf16[32,32,4]{2,0,1:T(8,128)(2,1)S(1)}, u32[]{:S(2)}) copy-start(bf16[32,32,4]{2,0,1:T(8,128)(2,1)S(1)} %collective-permute-done.4) | copy-start | bytes 24580
  87.0 6.7 collective-permute-start.6
  91.4 5.6 collective-permute-start.7
  100.4 24.8 %all-to-all-start = ((bf16[32,32,128]{2,1,0:T(8,128)(2,1)}), bf16[32,32,128]{2,1,0:T(8,128)(2,1)S(1)}, u32[]{:S(2)}, u32[]{:S(2)}) async-start(bf16[32,32,128]{2,1,0:T(8,128)(2,1)} %copy.103), calls=%async_computation | async-start | bytes 524288 | tf_op jit(solution)/shard_map/all_to_all | solution.py:66
  125.1 19.5 %all-to-all-start.7 = ((bf16[32,2,2048]{2,1,0:T(2,128)(2,1)}), bf16[32,2,2048]{2,1,0:T(2,128)(2,1)S(1)}, u32[]{:S(2)}, u32[]{:S(2)}) async-start(bf16[32,2,2048]{2,1,0:T(2,128)(2,1)} %reshape.152), calls=%async_computation.7 | async-start | bytes 524288 | tf_op jit(solution)/shard_map/all_to_all | solution.py:67
  144.6 15.1 %all-to-all-start.1 = ((bf16[32,2,2048]{2,1,0:T(2,128)(2,1)}), bf16[32,2,2048]{2,1,0:T(2,128)(2,1)S(1)}, u32[]{:S(2)}, u32[]{:S(2)}) async-start(bf16[32,2,2048]{2,1,0:T(2,128)(2,1)} %reshape.144), calls=%async_computation.1 | async-start | bytes 524288 | tf_op jit(solution)/shard_map/all_to_all | solution.py:67
  159.7 15.3 %all-to-all-start.8 = ((bf16[8,2,8192]{2,1,0:T(2,128)(2,1)}), bf16[8,2,8192]{2,1,0:T(2,128)(2,1)}, u32[]{:S(2)}, u32[]{:S(2)}) async-start(bf16[8,2,8192]{2,1,0:T(2,128)(2,1)} %reshape.154), calls=%async_computation.8 | async-start | bytes 524288 | tf_op jit(solution)/shard_map/all_to_all | solution.py:68
  175.1 42.2 %all-to-all-start.2 = ((bf16[8,2,8192]{2,1,0:T(2,128)(2,1)}), bf16[8,2,8192]{2,1,0:T(2,128)(2,1)}, u32[]{:S(2)}, u32[]{:S(2)}) async-start(bf16[8,2,8192]{2,1,0:T(2,128)(2,1)} %reshape.146), calls=%async_computation.2 | async-start | bytes 524288 | tf_op jit(solution)/shard_map/all_to_all | solution.py:68
  184.0 12.4 %collective-permute-start.16 = (bf16[32,32,8]{2,0,1:T(8,128)(2,1)S(1)}, bf16[32,32,8]{2,0,1:T(8,128)(2,1)S(1)}, u32[]{:S(2)}, u32[]{:S(2)}) collective-permute-start(bf16[32,32,8]{2,0,1:T(8,128)(2,1)S(1)} %get-tuple-element.72), channel_id=1, source_target_pairs={{0,32},{32,64},{64,96},{96,128},{128,160},{160,192},{192,224},{1,3... | collective-permute-start | bytes 49160 | tf_op jit(solution)/shard_map/ppermute | solution.py:15
  191.3 17.4 %collective-permute-start.17 = (bf16[32,32,8]{2,0,1:T(8,128)(2,1)S(1)}, bf16[32,32,8]{2,0,1:T(8,128)(2,1)S(1)}, u32[]{:S(2)}, u32[]{:S(2)}) collective-permute-start(bf16[32,32,8]{2,0,1:T(8,128)(2,1)S(1)} %get-tuple-element.73), channel_id=1, source_target_pairs={{32,0},{64,32},{96,64},{128,96},{160,128},{192,160},{224,192},{33,... | collective-permute-start | bytes 49160 | tf_op jit(solution)/shard_map/ppermute | solution.py:18
  209.6 24.2 %collective-permute-start.18 = (bf16[32,8,144]{2,0,1:T(8,128)(2,1)}, bf16[32,8,144]{2,0,1:T(8,128)(2,1)}, u32[]{:S(2)}, u32[]{:S(2)}) collective-permute-start(bf16[32,8,144]{2,0,1:T(8,128)(2,1)} %get-tuple-element.48), channel_id=1, source_target_pairs={{0,1},{1,2},{2,3},{3,4},{4,5},{5,6},{6,7},{7,8},{8,9},{9,10},{10,1... | collective-permute-start | bytes 221192 | tf_op jit(solution)/shard_map/ppermute | solution.py:15
  214.2 19.6 %collective-permute-start.19 = (bf16[32,8,144]{2,0,1:T(8,128)(2,1)}, bf16[32,8,144]{2,0,1:T(8,128)(2,1)}, u32[]{:S(2)}, u32[]{:S(2)}) collective-permute-start(bf16[32,8,144]{2,0,1:T(8,128)(2,1)} %get-tuple-element.49), channel_id=1, source_target_pairs={{1,0},{2,1},{3,2},{4,3},{5,4},{6,5},{7,6},{8,7},{9,8},{10,9},{11,1... | collective-permute-start | bytes 221192 | tf_op jit(solution)/shard_map/ppermute | solution.py:18
  221.1 16.0 %collective-permute-start.8 = (bf16[32,32,8]{2,0,1:T(8,128)(2,1)S(1)}, bf16[32,32,8]{2,0,1:T(8,128)(2,1)S(1)}, u32[]{:S(2)}, u32[]{:S(2)}) collective-permute-start(bf16[32,32,8]{2,0,1:T(8,128)(2,1)S(1)} %get-tuple-element.76), channel_id=1, source_target_pairs={{0,32},{32,64},{64,96},{96,128},{128,160},{160,192},{192,224},{1,3... | collective-permute-start | bytes 49160 | tf_op jit(solution)/shard_map/ppermute | solution.py:15
  232.3 16.4 %collective-permute-start.9 = (bf16[32,32,8]{2,0,1:T(8,128)(2,1)S(1)}, bf16[32,32,8]{2,0,1:T(8,128)(2,1)S(1)}, u32[]{:S(2)}, u32[]{:S(2)}) collective-permute-start(bf16[32,32,8]{2,0,1:T(8,128)(2,1)S(1)} %get-tuple-element.77), channel_id=1, source_target_pairs={{32,0},{64,32},{96,64},{128,96},{160,128},{192,160},{224,192},{33,... | collective-permute-start | bytes 49160 | tf_op jit(solution)/shard_map/ppermute | solution.py:18
  248.8 6.1 collective-permute-start.10
  252.7 6.3 collective-permute-start.11
  266.1 21.4 %collective-permute-start.20 = (bf16[32,32,8]{2,0,1:T(8,128)(2,1)S(1)}, bf16[32,32,8]{2,0,1:T(8,128)(2,1)S(1)}, u32[]{:S(2)}, u32[]{:S(2)}) collective-permute-start(bf16[32,32,8]{2,0,1:T(8,128)(2,1)S(1)} %get-tuple-element.70), channel_id=1, source_target_pairs={{0,32},{32,64},{64,96},{96,128},{128,160},{160,192},{192,224},{1,3... | collective-permute-start | bytes 49160 | tf_op jit(solution)/shard_map/ppermute | solution.py:15
  275.6 25.1 %collective-permute-start.21 = (bf16[32,32,8]{2,0,1:T(8,128)(2,1)S(1)}, bf16[32,32,8]{2,0,1:T(8,128)(2,1)S(1)}, u32[]{:S(2)}, u32[]{:S(2)}) collective-permute-start(bf16[32,32,8]{2,0,1:T(8,128)(2,1)S(1)} %get-tuple-element.71), channel_id=1, source_target_pairs={{32,0},{64,32},{96,64},{128,96},{160,128},{192,160},{224,192},{33,... | collective-permute-start | bytes 49160 | tf_op jit(solution)/shard_map/ppermute | solution.py:18
  276.9 29.2 %collective-permute-start.12 = (bf16[32,32,8]{2,0,1:T(8,128)(2,1)S(1)}, bf16[32,32,8]{2,0,1:T(8,128)(2,1)S(1)}, u32[]{:S(2)}, u32[]{:S(2)}) collective-permute-start(bf16[32,32,8]{2,0,1:T(8,128)(2,1)S(1)} %get-tuple-element.74), channel_id=1, source_target_pairs={{0,32},{32,64},{64,96},{96,128},{128,160},{160,192},{192,224},{1,3... | collective-permute-start | bytes 49160 | tf_op jit(solution)/shard_map/ppermute | solution.py:15
  284.8 25.1 %collective-permute-start.13 = (bf16[32,32,8]{2,0,1:T(8,128)(2,1)S(1)}, bf16[32,32,8]{2,0,1:T(8,128)(2,1)S(1)}, u32[]{:S(2)}, u32[]{:S(2)}) collective-permute-start(bf16[32,32,8]{2,0,1:T(8,128)(2,1)S(1)} %get-tuple-element.75), channel_id=1, source_target_pairs={{32,0},{64,32},{96,64},{128,96},{160,128},{192,160},{224,192},{33,... | collective-permute-start | bytes 49160 | tf_op jit(solution)/shard_map/ppermute | solution.py:18
  300.9 25.7 %collective-permute-start.22 = (bf16[32,8,144]{2,0,1:T(8,128)(2,1)S(1)}, bf16[32,8,144]{2,0,1:T(8,128)(2,1)S(1)}, u32[]{:S(2)}, u32[]{:S(2)}) collective-permute-start(bf16[32,8,144]{2,0,1:T(8,128)(2,1)S(1)} %get-tuple-element.44), channel_id=1, source_target_pairs={{0,1},{1,2},{2,3},{3,4},{4,5},{5,6},{6,7},{7,8},{8,9},{9,10},{10,1... | collective-permute-start | bytes 221192 | tf_op jit(solution)/shard_map/ppermute | solution.py:15
  304.2 22.4 %collective-permute-start.23 = (bf16[32,8,144]{2,0,1:T(8,128)(2,1)S(1)}, bf16[32,8,144]{2,0,1:T(8,128)(2,1)S(1)}, u32[]{:S(2)}, u32[]{:S(2)}) collective-permute-start(bf16[32,8,144]{2,0,1:T(8,128)(2,1)S(1)} %get-tuple-element.45), channel_id=1, source_target_pairs={{1,0},{2,1},{3,2},{4,3},{5,4},{6,5},{7,6},{8,7},{9,8},{10,9},{11,1... | collective-permute-start | bytes 221192 | tf_op jit(solution)/shard_map/ppermute | solution.py:18
  310.2 8.6 %collective-permute-start.14 = (bf16[32,8,144]{2,0,1:T(8,128)(2,1)S(1)}, bf16[32,8,144]{2,0,1:T(8,128)(2,1)S(1)}, u32[]{:S(2)}, u32[]{:S(2)}) collective-permute-start(bf16[32,8,144]{2,0,1:T(8,128)(2,1)S(1)} %get-tuple-element.52), channel_id=1, source_target_pairs={{0,1},{1,2},{2,3},{3,4},{4,5},{5,6},{6,7},{7,8},{8,9},{9,10},{10,1... | collective-permute-start | bytes 221192 | tf_op jit(solution)/shard_map/ppermute | solution.py:15
  315.4 6.3 collective-permute-start.15
  322.2 77.8 %copy-start.14 = (bf16[32,40,144]{2,0,1:T(8,128)(2,1)}, bf16[32,40,144]{2,0,1:T(8,128)(2,1)S(1)}, u32[]{:S(2)}) copy-start(bf16[32,40,144]{2,0,1:T(8,128)(2,1)S(1)} %get-tuple-element.51) | copy-start | bytes 1105924
  330.6 27.4 %all-to-all-start.9 = ((bf16[32,32,128]{2,1,0:T(8,128)(2,1)}), bf16[32,32,128]{2,1,0:T(8,128)(2,1)}, u32[]{:S(2)}, u32[]{:S(2)}) async-start(bf16[32,32,128]{2,1,0:T(8,128)(2,1)} %copy.126), calls=%async_computation.9 | async-start | bytes 524288 | tf_op jit(solution)/shard_map/all_to_all | solution.py:66
  358.0 14.4 %all-to-all-start.3 = ((bf16[32,32,128]{2,1,0:T(8,128)(2,1)}), bf16[32,32,128]{2,1,0:T(8,128)(2,1)}, u32[]{:S(2)}, u32[]{:S(2)}) async-start(bf16[32,32,128]{2,1,0:T(8,128)(2,1)} %copy.110), calls=%async_computation.3 | async-start | bytes 524288 | tf_op jit(solution)/shard_map/all_to_all | solution.py:66
  372.5 22.7 %all-to-all-start.10 = ((bf16[32,2,2048]{2,1,0:T(2,128)(2,1)}), bf16[32,2,2048]{2,1,0:T(2,128)(2,1)}, u32[]{:S(2)}, u32[]{:S(2)}) async-start(bf16[32,2,2048]{2,1,0:T(2,128)(2,1)} %reshape.156), calls=%async_computation.10 | async-start | bytes 524288 | tf_op jit(solution)/shard_map/all_to_all | solution.py:67
  395.1 15.7 %all-to-all-start.4 = ((bf16[32,2,2048]{2,1,0:T(2,128)(2,1)}), bf16[32,2,2048]{2,1,0:T(2,128)(2,1)}, u32[]{:S(2)}, u32[]{:S(2)}) async-start(bf16[32,2,2048]{2,1,0:T(2,128)(2,1)} %reshape.148), calls=%async_computation.4 | async-start | bytes 524288 | tf_op jit(solution)/shard_map/all_to_all | solution.py:67
  410.8 14.8 %all-to-all-start.11 = ((bf16[8,2,8192]{2,1,0:T(2,128)(2,1)}), bf16[8,2,8192]{2,1,0:T(2,128)(2,1)S(1)}, u32[]{:S(2)}, u32[]{:S(2)}) async-start(bf16[8,2,8192]{2,1,0:T(2,128)(2,1)} %reshape.158), calls=%async_computation.11 | async-start | bytes 524288 | tf_op jit(solution)/shard_map/all_to_all | solution.py:68
  425.6 16.1 %all-to-all-start.5 = ((bf16[8,2,8192]{2,1,0:T(2,128)(2,1)}), bf16[8,2,8192]{2,1,0:T(2,128)(2,1)S(1)}, u32[]{:S(2)}, u32[]{:S(2)}) async-start(bf16[8,2,8192]{2,1,0:T(2,128)(2,1)} %reshape.150), calls=%async_computation.5 | async-start | bytes 524288 | tf_op jit(solution)/shard_map/all_to_all | solution.py:68
  431.4 319.0 %all-reduce.3.cloned.1.call-start = ((), (), s32[]{:S(2)}) async-start(), calls=%async_computation.12 | async-start | bytes 1179648 | tf_op jit(solution)/shard_map/psum | solution.py:120
  444.1 9.2 %collective-permute-start.24 = (bf16[32,32,4]{2,0,1:T(8,128)(2,1)S(1)}, bf16[32,32,4]{2,0,1:T(8,128)(2,1)S(1)}, u32[]{:S(2)}, u32[]{:S(2)}) collective-permute-start(bf16[32,32,4]{2,0,1:T(8,128)(2,1)S(1)} %get-tuple-element.68), channel_id=1, source_target_pairs={{0,32},{32,64},{64,96},{96,128},{128,160},{160,192},{192,224},{1,3... | collective-permute-start | bytes 24584 | tf_op jit(solution)/shard_map/ppermute | solution.py:15
  446.7 19.5 %collective-permute-start.25 = (bf16[32,32,4]{2,0,1:T(8,128)(2,1)S(1)}, bf16[32,32,4]{2,0,1:T(8,128)(2,1)S(1)}, u32[]{:S(2)}, u32[]{:S(2)}) collective-permute-start(bf16[32,32,4]{2,0,1:T(8,128)(2,1)S(1)} %get-tuple-element.69), channel_id=1, source_target_pairs={{32,0},{64,32},{96,64},{128,96},{160,128},{192,160},{224,192},{33,... | collective-permute-start | bytes 24584 | tf_op jit(solution)/shard_map/ppermute | solution.py:18
  466.4 6.4 collective-permute-start.26
  470.4 5.6 collective-permute-start.27
  482.4 21.1 %collective-permute-start.28 = (bf16[32,32,4]{2,0,1:T(8,128)(2,1)S(1)}, bf16[32,32,4]{2,0,1:T(8,128)(2,1)S(1)}, u32[]{:S(2)}, u32[]{:S(2)}) collective-permute-start(bf16[32,32,4]{2,0,1:T(8,128)(2,1)S(1)} %get-tuple-element.66), channel_id=1, source_target_pairs={{0,32},{32,64},{64,96},{96,128},{128,160},{160,192},{192,224},{1,3... | collective-permute-start | bytes 24584 | tf_op jit(solution)/shard_map/ppermute | solution.py:15
  493.0 18.5 %collective-permute-start.29 = (bf16[32,32,4]{2,0,1:T(8,128)(2,1)S(1)}, bf16[32,32,4]{2,0,1:T(8,128)(2,1)S(1)}, u32[]{:S(2)}, u32[]{:S(2)}) collective-permute-start(bf16[32,32,4]{2,0,1:T(8,128)(2,1)S(1)} %get-tuple-element.67), channel_id=1, source_target_pairs={{32,0},{64,32},{96,64},{128,96},{160,128},{192,160},{224,192},{33,... | collective-permute-start | bytes 24584 | tf_op jit(solution)/shard_map/ppermute | solution.py:18
  511.7 4.6 collective-permute-start.30
  514.0 6.0 collective-permute-start.31
  (36 other events, 190.0 us)
Sparse Core Ops, SparseCore 0:
  495.8 254.5 all-reduce.2
where the time goes:
time: 774 us; the launch traced here: 764 us
  waiting for transfers between devices  415 us (54%)
  starting transfers between devices  220 us (28%)
  local copies, waits for them, and re-layouts  63.8 us (8%)
  matrix products  38.1 us (5%)
  between operations  16 us (2%)
  other arithmetic  10.3 us (1%)
    psum x1, waiting for transfers between devices, per_device(): lax.psum((kernel_grads[0], kernel_grads[1], kernel_grads[2], kernel_grads...  227 us
    ppermute x16, waiting for transfers between devices, padded_2(): lax.ppermute(lax.slice_in_dim(block, 0, width, axis=dim), axis, backward)  108 us
    ppermute x16, starting transfers between devices, padded_2(): lax.ppermute(lax.slice_in_dim(block, block.shape[dim] - width, None, axis...  100 us
    all_to_all x4, starting transfers between devices, mirror(): lax.all_to_all(field, 'row', split_axis=0, concat_axis=2, tiled=True)  46.9 us
    unnamed x109, local copies, waits for them, and re-layouts  41 us
    all_to_all x4, starting transfers between devices, mirror(): lax.all_to_all(spread, 'col', split_axis=2, concat_axis=1, tiled=True)  28.4 us
    dot_general x72, matrix products, apply_taps(): jnp.einsum('oi,irc->orc', kernel[row_tap, col_tap], shifted, preferred_el...  27.6 us
    all_to_all x4, waiting for transfers between devices, mirror(): lax.all_to_all(spread, 'col', split_axis=2, concat_axis=1, tiled=True)  27.6 us
  transfers between devices with their start and end apart: 45, of which 29 were waited for; matrix products, arithmetic and copies ran while one was open for 11% of the time, Pallas kernels for 0%

commit v1 on v0

v1 whole, which is shorter than its diff:
```python
import functools

import jax
import jax.numpy as jnp
from jax import lax
from jax.experimental import pallas as pl
from jax.experimental.pallas import tpu as pltpu
from jax.sharding import PartitionSpec as P

C = 32
BC = 32
BR = 128
DILATE_ONE = 4
DILATE_TWO = 8
MESH = pl.DeviceIdType.MESH
BF = jnp.bfloat16
F32 = jnp.float32


def dot(a, b):
    return jnp.dot(a, b, preferred_element_type=F32)


def permutation(inverse):
    row = lax.broadcasted_iota(jnp.int32, (256, 256), 0)
    col = lax.broadcasted_iota(jnp.int32, (256, 256), 1)
    if inverse:
        row, col = col, row
    same = (row // 8 == col % 32) & (row % 8 == col // 32)
    return jnp.where(same, 1.0, 0.0).astype(BF)


def fill_matrix(ref, row, kernel, flip, swap):
    for p in range(3):
        for q in range(3):
            a, b = (q, p) if swap else (p, q)
            if flip:
                piece = kernel[2 - a, 2 - b].astype(F32).T.astype(BF)
            else:
                piece = kernel[a, b]
            tap = 3 * p + q
            ref[row : row + C, tap * C : tap * C + C] = piece


def stack_shifts(v, d, lanes):
    return (
        pltpu.roll(v, d, 1)[:, :lanes],
        v[:, :lanes],
        pltpu.roll(v, 2 * BR - d, 1)[:, :lanes],
    )


def put_stack(ref, row, v, d, lanes):
    for q, part in enumerate(stack_shifts(v, d, lanes)):
        ref[row, q * C : q * C + C, :] = part


def taps(ref, row, d):
    return jnp.concatenate([ref[row], ref[row + d], ref[row + 2 * d]], axis=0)


def rows(count, body, unroll=8):
    def step(t, carry):
        for u in range(unroll):
            body(t * unroll + u)
        return carry

    lax.fori_loop(0, count // unroll, step, 0)


class Halo:
    names = ("own", "top", "bottom", "pack", "land", "send", "recv")

    def __init__(self, width, place, refs):
        self.h = width
        self.per = BR // width
        self.edge = 16 // self.per
        self.count = BC // self.per
        self.place = place
        self.own, self.top, self.bottom, self.pack, self.land, self.send, self.recv = refs

    @staticmethod
    def scratch(width):
        per = BR // width
        return [
            pltpu.VMEM((BC, C, BR), BF),
            pltpu.VMEM((width, C, BR), BF),
            pltpu.VMEM((width, C, BR), BF),
            pltpu.VMEM((2, BC // per, C, BR), BF),
            pltpu.VMEM((2, 64 // per, C, BR), BF),
            pltpu.SemaphoreType.DMA((8,)),
            pltpu.SemaphoreType.DMA((8,)),
        ]

    def pieces(self):
        e, n, h = self.edge, self.count, self.h
        return (
            (0, -1, self.own.at[0:h], self.bottom),
            (0, 1, self.own.at[BC - h : BC], self.top),
            (-1, 0, self.pack.at[0], self.land.at[0, e : e + n]),
            (1, 0, self.pack.at[1], self.land.at[1, e : e + n]),
            (-1, -1, self.pack.at[0, 0:e], self.land.at[0, e + n :]),
            (-1, 1, self.pack.at[0, n - e : n], self.land.at[0, 0:e]),
            (1, -1, self.pack.at[1, 0:e], self.land.at[1, e + n :]),
            (1, 1, self.pack.at[1, n - e : n], self.land.at[1, 0:e]),
        )

    def copy(self, k, piece):
        dr, dc, src, dst = piece
        return pltpu.make_async_remote_copy(
            src_ref=src,
            dst_ref=dst,
            send_sem=self.send.at[k],
            recv_sem=self.recv.at[k],
            device_id=(self.place.ri + dr, self.place.ci + dc),
            device_id_type=MESH,
        )

    def fill_edges(self):
        for dr, dc, src, dst in self.pieces():

            @pl.when(jnp.logical_not(self.place.inside(-dr, -dc)))
            def _():
                dst[...] = jnp.zeros(dst.shape, BF)

    def start(self):
        h, per = self.h, self.per
        group = lax.broadcasted_iota(jnp.int32, (C, BR), 1) // h

        def pack(t, carry):
            low = jnp.zeros((C, BR), BF)
            high = jnp.zeros((C, BR), BF)
            for j in range(per):
                v = self.own[t * per + j]
                low = jnp.where(group == j, pltpu.roll(v, j * h, 1), low)
                high = jnp.where(group == j, pltpu.roll(v, (j * h + h) % BR, 1), high)
            self.pack[0, t] = low
            self.pack[1, t] = high
            return carry

        lax.fori_loop(0, self.count, pack, 0)
        for k, piece in enumerate(self.pieces()):

            @pl.when(self.place.inside(piece[0], piece[1]))
            def _():
                self.copy(k, piece).start()

    def wait(self):
        for k, piece in enumerate(self.pieces()):

            @pl.when(self.place.inside(-piece[0], -piece[1]))
            def _():
                self.copy(k, piece).wait_recv()

    def drain(self):
        for k, piece in enumerate(self.pieces()):

            @pl.when(self.place.inside(piece[0], piece[1]))
            def _():
                self.copy(k, piece).wait_send()

    def build(self, ref, d):
        h, per, e = self.h, self.per, self.edge
        lane = lax.broadcasted_iota(jnp.int32, (C, BR), 1)

        def segment(main, first, pack, j0, nj, packs):
            def step(t, carry):
                low = self.land[0, pack + t]
                high = self.land[1, pack + t]
                for u in range(nj):
                    j = j0 + u
                    row = t * nj + u
                    side = jnp.where(
                        lane < h,
                        pltpu.roll(low, (BR - j * h) % BR, 1),
                        jnp.where(
                            lane >= BR - h,
                            pltpu.roll(high, (2 * BR - h - j * h) % BR, 1),
                            jnp.zeros((C, BR), BF),
                        ),
                    )
                    v = jnp.concatenate([main[row], side], axis=1)
                    put_stack(ref, first + row, v, d, 2 * BR)
                return carry

            lax.fori_loop(0, packs, step, 0)

        nj = min(per, h)
        segment(self.top, 0, 0, per - nj, nj, h // nj)
        segment(self.own, h, e, 0, per, BC // per)
        segment(self.bottom, h + BC, e + BC // per, 0, nj, h // nj)


class Mirror:
    def __init__(self, place, refs):
        self.place = place
        self.out, self.land, self.send, self.recv, self.local = refs

    @staticmethod
    def scratch():
        return [
            pltpu.VMEM((8, BR, BR), BF),
            pltpu.VMEM((4, 8, BC, BR), BF),
            pltpu.SemaphoreType.DMA((4,)),
            pltpu.SemaphoreType.DMA((4,)),
            pltpu.SemaphoreType.DMA,
        ]

    def target(self, k):
        return self.place.ci // 4, 4 * self.place.ri + k

    def is_self(self, k):
        row, col = self.target(k)
        return (row == self.place.ri) & (col == self.place.ci)

    def copy(self, k, slot):
        return pltpu.make_async_remote_copy(
            src_ref=self.out.at[:, k * BC : k * BC + BC],
            dst_ref=self.land.at[slot],
            send_sem=self.send.at[k],
            recv_sem=self.recv.at[slot],
            device_id=self.target(k),
            device_id_type=MESH,
        )

    def keep(self, k):
        return pltpu.make_async_copy(
            self.out.at[:, k * BC : k * BC + BC],
            self.land.at[lax.rem(self.place.ci, 4)],
            self.local,
        )

    def start(self):
        slot = lax.rem(self.place.ci, 4)
        for k in range(4):

            @pl.when(self.is_self(k))
            def _():
                self.keep(k).start()

            @pl.when(jnp.logical_not(self.is_self(k)))
            def _():
                self.copy(k, slot).start()

    def wait(self):
        for k in range(4):

            @pl.when(self.is_self(k))
            def _():
                self.keep(k).wait()

            @pl.when(jnp.logical_not(self.is_self(k)))
            def _():
                self.copy(k, k).wait_recv()

    def drain(self):
        for k in range(4):

            @pl.when(jnp.logical_not(self.is_self(k)))
            def _():
                self.copy(k, k).wait_send()

    def fetch(self):
        lane = lax.broadcasted_iota(jnp.int32, (8, BC, BR), 2)
        half = lane < 64
        even = (lane // 32) % 2 == 0
        l0, l1, l2, l3 = (self.land[k] for k in range(4))
        a0 = jnp.where(half, l0, pltpu.roll(l2, 64, 2))
        a2 = jnp.where(half, pltpu.roll(l0, 64, 2), l2)
        a1 = jnp.where(half, l1, pltpu.roll(l3, 64, 2))
        a3 = jnp.where(half, pltpu.roll(l1, 64, 2), l3)
        return (
            jnp.where(even, a0, pltpu.roll(a1, 32, 2)),
            jnp.where(even, pltpu.roll(a0, 96, 2), a1),
            jnp.where(even, a2, pltpu.roll(a3, 32, 2)),
            jnp.where(even, pltpu.roll(a2, 96, 2), a3),
        )


class Place:
    def __init__(self, nrow, ncol):
        self.nrow = nrow
        self.ncol = ncol
        self.ri = lax.axis_index("row")
        self.ci = lax.axis_index("col")

    def inside(self, dr, dc):
        ok = None
        for index, step, size in ((self.ri, dr, self.nrow), (self.ci, dc, self.ncol)):
            if step:
                here = index < size - 1 if step > 0 else index > 0
                ok = here if ok is None else ok & here
        return ok


def interleave(groups):
    return jnp.concatenate(groups, axis=1)


def kernel_grad(padding, own, stacked, d, out, first):
    padding[...] = jnp.zeros(padding.shape, BF)

    def fill(k):
        padding[k + 2 * d] = own(k)

    rows(BC, fill)

    def step(t, acc):
        left = []
        right = []
        for u in range(8):
            k = t * 8 + u
            left.append(
                jnp.concatenate([padding[k + 2 * d], padding[k + d], padding[k]], axis=0)
            )
            right.append(stacked[k, :, 0:BR])
        return acc + lax.dot_general(
            jnp.concatenate(left, axis=1),
            jnp.concatenate(right, axis=1),
            (((1,), (1,)), ((), ())),
            preferred_element_type=F32,
        )

    total = lax.fori_loop(0, (BC + 2 * d) // 8, step, jnp.zeros((3 * C, 3 * C), F32))
    per = out.shape[1]
    for t in range(3 * C // per):
        out[first * (3 * C) // per + t, :, 0 : 3 * C] = total[t * per : t * per + per]


SCRATCH_COUNT = {"halo": 7, "mirror": 5}


def main_kernel(nrow, ncol, *refs):
    (x_ref, g_ref, fa, fb, sa, sb, dec, g0, kg) = refs[:9]
    rest = list(refs[9:])

    def take(n):
        out = rest[:n]
        del rest[:n]
        return out

    place = Place(nrow, ncol)
    ri, ci = place.ri, place.ci
    halo_x = Halo(8, place, take(7))
    halo_s2 = Halo(16, place, take(7))
    halo_z = Halo(16, place, take(7))
    halo_s1 = Halo(8, place, take(7))
    mir_g = Mirror(place, take(5))
    mir_y = Mirror(place, take(5))
    (wa1, wb1, wa2, wb2, wb2t, tb2, ta2, ta2t, tb1, ta1) = take(10)
    (xc1, hc1, slope1, xc2, sc2, hg2, hc2, hc2t, ec2, ec2t, sc1, ec1, y1, e2own, e1own) = take(15)
    (pad, acc, r1, mine, r2, fin, s1_send, s1_recv, s2_send, s2_recv, s3_send, s3_recv) = take(12)
    halos = (halo_x, halo_s2, halo_z, halo_s1)

    n1 = ncol // 2
    n2 = 2 * nrow
    a = lax.rem(ci, n1)
    half = ci // n1
    me2 = ri * 2 + half

    def group1(b):
        return ri, half * n1 + b

    def group2(m):
        return m // 2, lax.rem(m, 2) * n1 + a

    barrier = pltpu.get_barrier_semaphore()
    expected = jnp.int32(n1 + n2 - 2)

    def greet(row, col):
        pl.semaphore_signal(barrier, inc=1, device_id=(row, col), device_id_type=MESH)

    for dr in (-1, 0, 1):
        for dc in (-1, 0, 1):
            if dr or dc:
                ok = place.inside(dr, dc)
                expected = expected + ok.astype(jnp.int32)

                @pl.when(ok)
                def _():
                    greet(ri + dr, ci + dc)

    for k in range(4):
        away = jnp.logical_not(mir_g.is_self(k))
        expected = expected + away.astype(jnp.int32)

        @pl.when(away)
        def _():
            greet(*mir_g.target(k))

    def greet1(b, carry):
        @pl.when(b != a)
        def _():
            greet(*group1(b))

        return carry

    def greet2(m, carry):
        @pl.when(m != me2)
        def _():
            greet(*group2(m))

        return carry

    lax.fori_loop(0, n1, greet1, 0)
    lax.fori_loop(0, n2, greet2, 0)

    order = permutation(False)
    flat = x_ref[...].reshape(C * BC, BR)
    halo_x.own[...] = interleave(
        [dot(order, flat[256 * t : 256 * t + 256]).reshape(BC, 8, BR) for t in range(4)]
    ).astype(BF)
    gflat = g_ref[...].reshape(C * BC, BR)
    for j in range(8):
        mir_g.out[j] = gflat[j * BR : j * BR + BR].T
    for halo in halos:
        halo.fill_edges()
    pl.semaphore_wait(barrier, expected)
    halo_x.start()
    mir_g.start()

    fill_matrix(wa1, 0, fa, False, False)
    fill_matrix(wb1, 0, fb, False, False)
    fill_matrix(wa2, 0, sa, False, False)
    fill_matrix(wa2, C, sa, False, True)
    fill_matrix(wb2, 0, sb, False, False)
    fill_matrix(wb2t, 0, sb, False, True)
    fill_matrix(tb2, 0, sb, True, False)
    fill_matrix(tb2, C, sb, True, True)
    fill_matrix(ta2, 0, sa, True, False)
    fill_matrix(ta2t, 0, sa, True, True)
    fill_matrix(tb1, 0, fb, True, False)
    fill_matrix(ta1, 0, fa, True, False)

    lane = lax.broadcasted_iota(jnp.int32, (C, 2 * BR), 1)
    first_lane = jnp.where(ri < nrow - 1, BR, BR + 64)
    last_lane = jnp.where(ri > 0, 2 * BR, BR + 64)
    lane_ok = (lane < BR) | ((lane >= first_lane) & (lane < last_lane))

    def on_map(row, v):
        bin_index = ci * BC + row
        ok = (bin_index >= 0) & (bin_index < ncol * BC)
        return jnp.where(lane_ok & ok, v, 0.0)

    d = DILATE_ONE
    halo_x.wait()
    halo_x.build(xc1, d)

    def hidden1(k):
        pre = dot(wa1[...], taps(xc1, k, d))
        sig = jax.nn.sigmoid(pre)
        slope1[k] = sig * (1.0 + pre * (1.0 - sig))
        put_stack(hc1, k, on_map(k - d, pre * sig).astype(BF), d, BR)

    rows(BC + 2 * d, hidden1)

    def outer1(k):
        y1[k] = (halo_x.own[k].astype(F32) + dot(wb1[...], taps(hc1, k, d))).astype(BF)

    rows(BC, outer1)

    back = permutation(True)
    for t in range(4):
        part = y1[:, 8 * t : 8 * t + 8, :].reshape(256, BR)
        natural = dot(back, part)
        for j in range(2):
            mir_y.out[2 * t + j] = natural[j * BR : j * BR + BR].T.astype(BF)
    mir_y.start()

    mir_g.wait()
    turned = mir_g.fetch()
    parts = []
    for t in range(4):
        mirrored = jnp.concatenate(
            [turned[n][2 * t + j] for j in range(2) for n in range(4)], axis=0
        )
        here = gflat[256 * t : 256 * t + 256]
        mean = ((here.astype(F32) + mirrored.astype(F32)) * 0.5).astype(BF)
        parts.append(dot(order, mean).reshape(BC, 8, BR))
    halo_s2.own[...] = interleave(parts).astype(BF)
    halo_s2.start()

    mir_y.wait()
    turned = mir_y.fetch()
    parts = []
    for t in range(4):
        mirrored = jnp.concatenate(
            [turned[n][2 * t + j] for j in range(2) for n in range(4)], axis=0
        )
        parts.append(dot(order, mirrored).reshape(BC, 8, BR))
    halo_z.own[...] = ((y1[...].astype(F32) + interleave(parts)) * 0.5).astype(BF)
    halo_z.start()

    d = DILATE_TWO
    halo_s2.wait()
    halo_s2.build(sc2, d)

    def cotangent2(k):
        hg2[k] = dot(tb2[...], taps(sc2, k, d))

    rows(BC + 2 * d, cotangent2)
    halo_z.wait()
    halo_z.build(xc2, d)

    def hidden2(k):
        pre = dot(wa2[...], taps(xc2, k, d))
        sig = jax.nn.sigmoid(pre)
        hid = pre * sig
        grad = hg2[k] * (sig * (1.0 + pre * (1.0 - sig)))
        put_stack(hc2, k, on_map(k - d, hid[:C]).astype(BF), d, BR)
        put_stack(hc2t, k, on_map(k - d, hid[C:]).astype(BF), d, BR)
        put_stack(ec2, k, on_map(k - d, grad[:C]).astype(BF), d, BR)
        put_stack(ec2t, k, on_map(k - d, grad[C:]).astype(BF), d, BR)

    rows(BC + 2 * d, hidden2, 4)

    def upstream1(k):
        base = halo_s2.own[k].astype(F32)
        one = (base + dot(ta2[...], taps(ec2, k, d))).astype(BF)
        two = (base + dot(ta2t[...], taps(ec2t, k, d))).astype(BF)
        halo_s1.own[k] = ((one.astype(F32) + two.astype(F32)) * 0.5).astype(BF)

    rows(BC, upstream1)
    halo_s1.start()

    def outer2(k):
        base = halo_z.own[k].astype(F32)
        one = (base + dot(wb2[...], taps(hc2, k, d))).astype(BF)
        two = (base + dot(wb2t[...], taps(hc2t, k, d))).astype(BF)
        dec[k] = ((one.astype(F32) + two.astype(F32)) * 0.5).astype(BF)

    rows(BC, outer2)
    acc[...] = jnp.zeros(acc.shape, F32)
    kernel_grad(pad.at[0 : BC + 4 * d], lambda k: halo_s2.own[k], hc2, d, acc, 3)
    kernel_grad(
        pad.at[0 : BC + 4 * d], lambda k: ec2[k + DILATE_TWO, C : 2 * C, :], xc2.at[d : d + BC + 2 * d], d, acc, 2
    )

    d = DILATE_ONE
    kernel_grad(pad.at[0 : BC + 4 * d], lambda k: halo_s1.own[k], hc1, d, acc, 1)
    halo_s1.wait()
    halo_s1.build(sc1, d)

    def cotangent1(k):
        grad = dot(tb1[...], taps(sc1, k, d)) * slope1[k]
        put_stack(ec1, k, on_map(k - d, grad).astype(BF), d, BR)

    rows(BC + 2 * d, cotangent1)
    kernel_grad(
        pad.at[0 : BC + 4 * d], lambda k: ec1[k + DILATE_ONE, C : 2 * C, :], xc1.at[d : d + BC + 2 * d], d, acc, 0
    )

    def share(src, dst, send, recv, slot, device):
        return pltpu.make_async_remote_copy(
            src_ref=src, dst_ref=dst, send_sem=send, recv_sem=recv, device_id=device, device_id_type=MESH
        )

    def others(count, me, body):
        def step(b, carry):
            @pl.when(b != me)
            def _():
                body(b)

            return carry

        lax.fori_loop(0, count, step, 0)

    def scatter(b, slot):
        return share(acc.at[b], r1.at[slot], s1_send.at[b], s1_recv.at[slot], slot, group1(b))

    def spread(m, slot):
        return share(mine, r2.at[slot], s2_send.at[m], s2_recv.at[slot], slot, group2(m))

    def gather(b, slot):
        return share(fin.at[a], fin.at[slot], s3_send.at[b], s3_recv.at[slot], slot, group1(b))

    others(n1, a, lambda b: scatter(b, a).start())

    def upstream0(k):
        g0[k] = (halo_s1.own[k].astype(F32) + dot(ta1[...], taps(ec1, k, d))).astype(BF)

    rows(BC, upstream0)
    r1[a] = acc[a]
    others(n1, a, lambda b: scatter(b, b).wait_recv())
    mine[...] = lax.fori_loop(1, n1, lambda b, total: total + r1[b], r1[0])
    others(n2, me2, lambda m: spread(m, me2).start())
    r2[me2] = mine[...]
    others(n2, me2, lambda m: spread(m, m).wait_recv())
    fin[a] = lax.fori_loop(1, n2, lambda m, total: total + r2[m], r2[0])
    others(n1, a, lambda b: gather(b, a).start())
    for halo in halos:
        halo.drain()
    mir_g.drain()
    mir_y.drain()
    others(n1, a, lambda b: scatter(b, a).wait_send())
    others(n2, me2, lambda m: spread(m, me2).wait_send())
    others(n1, a, lambda b: gather(b, b).wait_recv())
    others(n1, a, lambda b: gather(b, a).wait_send())
    kg[...] = fin[...].reshape(kg.shape)


def finish_kernel(dec, g0, kg, out_dec, out_g0, out_a1, out_b1, out_a2, out_b2):
    back = permutation(True)
    for src, dst in ((dec, out_dec), (g0, out_g0)):
        whole = src[...].astype(F32)
        for t in range(4):
            part = whole[:, 8 * t : 8 * t + 8, :].reshape(256, BR).astype(BF)
            dst[8 * t : 8 * t + 8] = dot(back, part).astype(BF).reshape(8, BC, BR)
    for k, dst in enumerate((out_a1, out_b1, out_a2, out_b2)):
        for p in range(3):
            band = kg[(3 * k + p) * C : (3 * k + p) * C + C, :]
            for q in range(3):
                dst[p, q] = band[:, q * C : q * C + C]


def per_device(nrow, ncol, pair_map, out_grad, first_a, first_b, second_a, second_b):
    n1 = ncol // 2
    n2 = 2 * nrow
    per = 12 * C // n1
    wide = BC + 16
    vmem = pltpu.VMEM
    scratch = (
        Halo.scratch(8)
        + Halo.scratch(16)
        + Halo.scratch(16)
        + Halo.scratch(8)
        + Mirror.scratch()
        + Mirror.scratch()
        + [vmem((m, 9 * C), BF) for m in (C, C, 2 * C, C, C, 2 * C, C, C, C, C)]
        + [
            vmem((BC + 16, 3 * C, 2 * BR), BF),
            vmem((BC + 8, 3 * C, BR), BF),
            vmem((BC + 8, C, 2 * BR), F32),
            vmem((BC + 32, 3 * C, 2 * BR), BF),
            vmem((BC + 32, 3 * C, 2 * BR), BF),
            vmem((wide, 2 * C, 2 * BR), F32),
            vmem((wide, 3 * C, BR), BF),
            vmem((wide, 3 * C, BR), BF),
            vmem((wide, 3 * C, BR), BF),
            vmem((wide, 3 * C, BR), BF),
            vmem((BC + 16, 3 * C, 2 * BR), BF),
            vmem((BC + 8, 3 * C, BR), BF),
            vmem((BC, C, BR), BF),
            vmem((8, BR), F32),
            vmem((8, BR), F32),
        ]
        + [
            vmem((BC + 32, C, BR), BF),
            vmem((n1, per, BR), F32),
            vmem((n1, per, BR), F32),
            vmem((per, BR), F32),
            vmem((n2, per, BR), F32),
            vmem((n1, per, BR), F32),
        ]
        + [pltpu.SemaphoreType.DMA((n,)) for n in (n1, n1, n2, n2, n1, n1)]
    )
    whole = pl.BlockSpec(memory_space=pltpu.VMEM)
    dec, g0, kg = pl.pallas_call(
        functools.partial(main_kernel, nrow, ncol),
        out_shape=[
            jax.ShapeDtypeStruct((BC, C, BR), BF),
            jax.ShapeDtypeStruct((BC, C, BR), BF),
            jax.ShapeDtypeStruct((12 * C, BR), F32),
        ],
        in_specs=[whole] * 6,
        out_specs=[whole] * 3,
        scratch_shapes=scratch,
        compiler_params=pltpu.CompilerParams(
            collective_id=0, has_side_effects=True, vmem_limit_bytes=56 << 20
        ),
        name="blocks",
    )(pair_map, out_grad, first_a, first_b, second_a, second_b)
    small = jax.ShapeDtypeStruct((3, 3, C, C), F32)
    return pl.pallas_call(
        finish_kernel,
        out_shape=[
            jax.ShapeDtypeStruct((C, BC, BR), BF),
            jax.ShapeDtypeStruct((C, BC, BR), BF),
            small,
            small,
            small,
            small,
        ],
        in_specs=[whole] * 3,
        out_specs=[whole] * 6,
        compiler_params=pltpu.CompilerParams(vmem_limit_bytes=24 << 20),
        name="finish",
    )(dec, g0, kg)


def solution(mesh):
    return jax.shard_map(
        functools.partial(per_device, mesh.shape["row"], mesh.shape["col"]),
        mesh=mesh,
        in_specs=(P(None, "col", "row"), P(None, "col", "row"), P(), P(), P(), P()),
        out_specs=(P(None, "col", "row"), P(None, "col", "row"), P(), P(), P(), P()),
        check_vma=False,
    )
```

time: 774 us -> 126 us (0.16); the launches traced: 764 us -> 126 us
  waiting for transfers between devices: 415 us -> 0 us
  starting transfers between devices: 220 us -> 0 us
  Pallas kernels: 0 us -> 122 us
  local copies, waits for them, and re-layouts: 63.8 us -> 2.82 us
  matrix products: 38.1 us -> 0 us
  between operations: 16 us -> 0.65 us
  other arithmetic: 10.3 us -> 0 us
    psum x1 -> x0, waiting for transfers between devices: 227 us -> none  [per_device(): lax.psum((kernel_grads[0], kernel_grads[1], kernel_grads[2], kernel_grads...]
    ppermute x32 -> x0, waiting for transfers between devices: 128 us -> none  [the longest x16 108 us: padded_2(): lax.ppermute(lax.slice_in_dim(block, 0, width, axis=dim), axis, backward)]
    ppermute x32 -> x0, starting transfers between devices: 127 us -> none  [the longest x16 100 us: padded_2(): lax.ppermute(lax.slice_in_dim(block, block.shape[dim] - width, None, axis...]
    pallas_call x0 -> x2, Pallas kernels: none -> 122 us  [the longest x1 121 us: per_device(): pl.pallas_call(functools.partial(main_kernel, nrow, ncol), out_shape=[jax...]
    all_to_all x12 -> x0, starting transfers between devices: 93.5 us -> none  [the longest x4 46.9 us: mirror(): lax.all_to_all(field, 'row', split_axis=0, concat_axis=2, tiled=True)]
    all_to_all x12 -> x0, waiting for transfers between devices: 60.4 us -> none  [the longest x4 27.6 us: mirror(): lax.all_to_all(spread, 'col', split_axis=2, concat_axis=1, tiled=True)]
    unnamed x109 -> x6, local copies, waits for them, and re-layouts: 41 us -> 2.82 us
    dot_general x108 -> x0, matrix products: 38.1 us -> none  [the longest x72 27.6 us: apply_taps(): jnp.einsum('oi,irc->orc', kernel[row_tap, col_tap], shifted, preferred_el...]
  transfers between devices with their start and end apart: 45 -> 0, of which waited for: 29 -> 0; matrix products, arithmetic and copies ran while one was open for 11% -> 0% of each run, Pallas kernels for 0% -> 0%
where the time goes in v1:
time: 126 us
  Pallas kernels  122 us (97%)
  local copies, waits for them, and re-layouts  2.82 us (2%)
    pallas_call x1, Pallas kernels, per_device(): pl.pallas_call(functools.partial(main_kernel, nrow, ncol), out_shape=[jax...  121 us
    unnamed x6, local copies, waits for them, and re-layouts  2.82 us

profile of v1, /device:TPU:1, one launch (start us, length us, event | category | flops | bytes accessed | tf_op | source)
XLA Modules:
  0.0 125.6 jit_solution(7492429565764990352)
XLA Ops:
  0.6 120.8 %blocks.1 = (bf16[32,32,128]{2,1,0:T(8,128)(2,1)}, bf16[32,32,128]{2,1,0:T(8,128)(2,1)}, f32[384,128]{1,0:T(8,128)}) custom-call(bf16[32,32,128]{2,1,0:T(8,128)(2,1)} %refs_0_.1, bf16[32,32,128]{2,1,0:T(8,128)(2,1)} %refs_1_.1, bf16[3,3,32,32]{3,2,1,0:T(8,128)(2,1)} %refs_2_.1, bf16[3,3,32,32]{3,2,1,0:T(8,128)(2,1)} %refs_3_.1, ...), custom_call_target="tpu_custom_call" | custom-call | tf_op jit(solution)/shard_map/blocks/pallas_call | solution.py:658
  121.5 0.0 copy-start
  121.5 0.9 copy-done
  122.4 0.0 copy-start.1
  122.4 0.9 copy-done.1
  123.4 0.0 copy-start.2
  123.4 0.9 copy-done.2
  124.3 1.3 %finish.1 = (bf16[32,32,128]{2,1,0:T(8,128)(2,1)}, bf16[32,32,128]{2,1,0:T(8,128)(2,1)}, f32[3,3,32,32]{3,2,1,0:T(8,128)}, f32[3,3,32,32]{3,2,1,0:T(8,128)}, f32...) custom-call(bf16[32,32,128]{2,1,0:T(8,128)(2,1)S(1)} %copy-done, bf16[32,32,128]{2,1,0:T(8,128)(2,1)S(1)} %copy-done.1, ...), custom_call_target="tpu_custom_call" | custom-call | tf_op jit(solution)/shard_map/finish/pallas_call | solution.py:674
Async XLA Ops:
  121.5 1.0 copy-start
  122.4 0.9 copy-start.1
  123.4 0.9 copy-start.2

commit v2 on v1

--- a/solution.py
+++ b/solution.py
@@ -194,71 +194,144 @@
 class Mirror:
     def __init__(self, place, refs):
         self.place = place
-        self.out, self.land, self.send, self.recv, self.local = refs
+        self.n = place.nrow
+        self.per = 8 // place.nrow
+        self.ri = place.ri
+        self.cq = place.ci // 4
+        self.s = lax.rem(place.ci, 4)
+        self.out, self.relay, self.land, self.send1, self.recv1, self.send2, self.recv2 = refs
 
     @staticmethod
-    def scratch():
+    def scratch(nrow):
         return [
             pltpu.VMEM((8, BR, BR), BF),
+            pltpu.VMEM((nrow, 8 // nrow, BR, BR), BF),
             pltpu.VMEM((4, 8, BC, BR), BF),
-            pltpu.SemaphoreType.DMA((4,)),
-            pltpu.SemaphoreType.DMA((4,)),
-            pltpu.SemaphoreType.DMA,
+            pltpu.SemaphoreType.DMA((nrow,)),
+            pltpu.SemaphoreType.DMA((nrow,)),
+            pltpu.SemaphoreType.DMA((nrow, 4)),
+            pltpu.SemaphoreType.DMA((4, nrow)),
         ]
 
-    def target(self, k):
-        return self.place.ci // 4, 4 * self.place.ri + k
-
-    def is_self(self, k):
-        row, col = self.target(k)
-        return (row == self.place.ri) & (col == self.place.ci)
-
-    def copy(self, k, slot):
+    def relay_of(self, ri, cq, s, q):
+        return 2 * (q // 2) + lax.rem(ri, 2), 4 * (2 * (cq // 2) + lax.rem(q, 2)) + s
+
+    def source(self, w):
+        return 2 * (w // 2) + lax.rem(self.ri, 2), 2 * (self.cq // 2) + lax.rem(w, 2)
+
+    def my_w(self):
+        return 2 * (self.ri // 2) + lax.rem(self.cq, 2)
+
+    def my_q(self):
+        return 2 * (self.ri // 2) + lax.rem(self.cq, 2)
+
+    def first(self, q, w):
+        return self.out.at[pl.ds(q * self.per, self.per)], self.relay.at[w], self.recv1.at[w]
+
+    def second(self, w, k, slot, q):
+        r0 = pl.multiple_of(k * BC, BC)
+        return (
+            self.relay.at[w, :, pl.ds(r0, BC)],
+            self.land.at[slot, pl.ds(q * self.per, self.per)],
+            self.recv2.at[slot, q],
+        )
+
+    def target1(self, q):
+        return self.relay_of(self.ri, self.cq, self.s, q)
+
+    def target2(self, w, k):
+        ri, cq = self.source(w)
+        return cq, 4 * ri + k
+
+    def is_self(self, device):
+        return (device[0] == self.ri) & (device[1] == self.place.ci)
+
+    def copy(self, parts, send, device):
+        src, dst, recv = parts
         return pltpu.make_async_remote_copy(
-            src_ref=self.out.at[:, k * BC : k * BC + BC],
-            dst_ref=self.land.at[slot],
-            send_sem=self.send.at[k],
-            recv_sem=self.recv.at[slot],
-            device_id=self.target(k),
-            device_id_type=MESH,
-        )
-
-    def keep(self, k):
-        return pltpu.make_async_copy(
-            self.out.at[:, k * BC : k * BC + BC],
-            self.land.at[lax.rem(self.place.ci, 4)],
-            self.local,
-        )
+            src_ref=src, dst_ref=dst, send_sem=send, recv_sem=recv, device_id=device, device_id_type=MESH
+        )
+
+    def go(self, parts, send, device):
+        here = self.is_self(device)
+
+        @pl.when(here)
+        def _():
+            pltpu.make_async_copy(*parts).start()
+
+        @pl.when(jnp.logical_not(here))
+        def _():
+            self.copy(parts, send, device).start()
+
+    def arrived(self, parts, send):
+        self.copy(parts, send, (self.ri, self.place.ci)).wait_recv()
 
     def start(self):
-        slot = lax.rem(self.place.ci, 4)
-        for k in range(4):
-
-            @pl.when(self.is_self(k))
+        w = self.my_w()
+
+        def step(q, carry):
+            self.go(self.first(q, w), self.send1.at[q], self.target1(q))
+            return carry
+
+        lax.fori_loop(0, self.n, step, 0)
+
+    def forward(self):
+        mine = self.my_q()
+
+        def step(w, carry):
+            self.arrived(self.first(0, w), self.send1.at[0])
+            for k in range(4):
+                self.go(self.second(w, k, self.s, mine), self.send2.at[w, k], self.target2(w, k))
+            return carry
+
+        lax.fori_loop(0, self.n, step, 0)
+
+    def wait(self):
+        def step(q, carry):
+            for k in range(4):
+                self.arrived(self.second(0, 0, k, q), self.send2.at[0, 0])
+            return carry
+
+        lax.fori_loop(0, self.n, step, 0)
+
+    def drain(self):
+        def step(q, carry):
+            @pl.when(jnp.logical_not(self.is_self(self.target1(q))))
             def _():
-                self.keep(k).start()
-
-            @pl.when(jnp.logical_not(self.is_self(k)))
+                self.copy(self.first(q, 0), self.send1.at[q], self.target1(q)).wait_send()
+
+            for k in range(4):
+
+                @pl.when(jnp.logical_not(self.is_self(self.target2(q, k))))
+                def _():
+                    self.copy(self.second(q, k, 0, 0), self.send2.at[q, k], self.target2(q, k)).wait_send()
+
+            return carry
+
+        lax.fori_loop(0, self.n, step, 0)
+
+    def greet(self, greet):
+        def step(q, count):
+            ri, cq = self.source(q)
+            source = ri, 4 * cq + self.s
+
+            @pl.when(jnp.logical_not(self.is_self(source)))
             def _():
-                self.copy(k, slot).start()
-
-    def wait(self):
-        for k in range(4):
-
-            @pl.when(self.is_self(k))
-            def _():
-                self.keep(k).wait()
-
-            @pl.when(jnp.logical_not(self.is_self(k)))
-            def _():
-                self.copy(k, k).wait_recv()
-
-    def drain(self):
-        for k in range(4):
-
-            @pl.when(jnp.logical_not(self.is_self(k)))
-            def _():
-                self.copy(k, k).wait_send()
+                greet(*source)
+
+            count = count + jnp.logical_not(self.is_self(self.target1(q))).astype(jnp.int32)
+            for k in range(4):
+                relay = self.relay_of(self.cq, self.ri, k, q)
+
+                @pl.when(jnp.logical_not(self.is_self(relay)))
+                def _():
+                    greet(*relay)
+
+                away = jnp.logical_not(self.is_self(self.target2(q, k)))
+                count = count + away.astype(jnp.int32)
+            return count
+
+        return lax.fori_loop(0, self.n, step, jnp.int32(0))
 
     def fetch(self):
         lane = lax.broadcasted_iota(jnp.int32, (8, BC, BR), 2)
@@ -327,9 +400,6 @@
         out[first * (3 * C) // per + t, :, 0 : 3 * C] = total[t * per : t * per + per]
 
 
-SCRATCH_COUNT = {"halo": 7, "mirror": 5}
-
-
 def main_kernel(nrow, ncol, *refs):
     (x_ref, g_ref, fa, fb, sa, sb, dec, g0, kg) = refs[:9]
     rest = list(refs[9:])
@@ -345,8 +415,8 @@
     halo_s2 = Halo(16, place, take(7))
     halo_z = Halo(16, place, take(7))
     halo_s1 = Halo(8, place, take(7))
-    mir_g = Mirror(place, take(5))
-    mir_y = Mirror(place, take(5))
+    mir_g = Mirror(place, take(7))
+    mir_y = Mirror(place, take(7))
     (wa1, wb1, wa2, wb2, wb2t, tb2, ta2, ta2t, tb1, ta1) = take(10)
     (xc1, hc1, slope1, xc2, sc2, hg2, hc2, hc2t, ec2, ec2t, sc1, ec1, y1, e2own, e1own) = take(15)
     (pad, acc, r1, mine, r2, fin, s1_send, s1_recv, s2_send, s2_recv, s3_send, s3_recv) = take(12)
@@ -380,13 +450,7 @@
                 def _():
                     greet(ri + dr, ci + dc)
 
-    for k in range(4):
-        away = jnp.logical_not(mir_g.is_self(k))
-        expected = expected + away.astype(jnp.int32)
-
-        @pl.when(away)
-        def _():
-            greet(*mir_g.target(k))
+    expected = expected + mir_g.greet(greet)
 
     def greet1(b, carry):
         @pl.when(b != a)
@@ -453,6 +517,7 @@
         put_stack(hc1, k, on_map(k - d, pre * sig).astype(BF), d, BR)
 
     rows(BC + 2 * d, hidden1)
+    mir_g.forward()
 
     def outer1(k):
         y1[k] = (halo_x.own[k].astype(F32) + dot(wb1[...], taps(hc1, k, d))).astype(BF)
@@ -479,6 +544,7 @@
         parts.append(dot(order, mean).reshape(BC, 8, BR))
     halo_s2.own[...] = interleave(parts).astype(BF)
     halo_s2.start()
+    mir_y.forward()
 
     mir_y.wait()
     turned = mir_y.fetch()
@@ -624,8 +690,8 @@
         + Halo.scratch(16)
         + Halo.scratch(16)
         + Halo.scratch(8)
-        + Mirror.scratch()
-        + Mirror.scratch()
+        + Mirror.scratch(nrow)
+        + Mirror.scratch(nrow)
         + [vmem((m, 9 * C), BF) for m in (C, C, 2 * C, C, C, 2 * C, C, C, C, C)]
         + [
             vmem((BC + 16, 3 * C, 2 * BR), BF),

time: 126 us -> 108 us (0.86)
  Pallas kernels: 122 us -> 104 us
    pallas_call x1, Pallas kernels: 121 us -> 103 us  [per_device(): pl.pallas_call(functools.partial(main_kernel, nrow, ncol), out_shape=[jax...]
where the time goes in v2:
time: 108 us
  Pallas kernels  104 us (96%)
  local copies, waits for them, and re-layouts  2.82 us (3%)
    pallas_call x1, Pallas kernels, per_device(): pl.pallas_call(functools.partial(main_kernel, nrow, ncol), out_shape=[jax...  103 us
    unnamed x6, local copies, waits for them, and re-layouts  2.82 us

profile of v2, /device:TPU:1, one launch (start us, length us, event | category | flops | bytes accessed | tf_op | source)
XLA Modules:
  0.0 107.7 jit_solution(6812318644725554350)
XLA Ops:
  0.6 103.0 %blocks.1 = (bf16[32,32,128]{2,1,0:T(8,128)(2,1)}, bf16[32,32,128]{2,1,0:T(8,128)(2,1)}, f32[384,128]{1,0:T(8,128)}) custom-call(bf16[32,32,128]{2,1,0:T(8,128)(2,1)} %refs_0_.1, bf16[32,32,128]{2,1,0:T(8,128)(2,1)} %refs_1_.1, bf16[3,3,32,32]{3,2,1,0:T(8,128)(2,1)} %refs_2_.1, bf16[3,3,32,32]{3,2,1,0:T(8,128)(2,1)} %refs_3_.1, ...), custom_call_target="tpu_custom_call" | custom-call | tf_op jit(solution)/shard_map/blocks/pallas_call | solution.py:724
  103.6 0.0 copy-start
  103.6 0.9 copy-done
  104.6 0.0 copy-start.1
  104.6 0.9 copy-done.1
  105.5 0.0 copy-start.2
  105.5 0.9 copy-done.2
  106.5 1.3 %finish.1 = (bf16[32,32,128]{2,1,0:T(8,128)(2,1)}, bf16[32,32,128]{2,1,0:T(8,128)(2,1)}, f32[3,3,32,32]{3,2,1,0:T(8,128)}, f32[3,3,32,32]{3,2,1,0:T(8,128)}, f32...) custom-call(bf16[32,32,128]{2,1,0:T(8,128)(2,1)S(1)} %copy-done, bf16[32,32,128]{2,1,0:T(8,128)(2,1)S(1)} %copy-done.1, ...), custom_call_target="tpu_custom_call" | custom-call | tf_op jit(solution)/shard_map/finish/pallas_call | solution.py:740
Async XLA Ops:
  103.6 1.0 copy-start
  104.6 0.9 copy-start.1
  105.5 0.9 copy-start.2

commit v3 on v2

--- a/solution.py
+++ b/solution.py
@@ -42,17 +42,17 @@
             ref[row : row + C, tap * C : tap * C + C] = piece
 
 
-def stack_shifts(v, d, lanes):
-    return (
-        pltpu.roll(v, d, 1)[:, :lanes],
-        v[:, :lanes],
-        pltpu.roll(v, 2 * BR - d, 1)[:, :lanes],
-    )
-
-
-def put_stack(ref, row, v, d, lanes):
-    for q, part in enumerate(stack_shifts(v, d, lanes)):
-        ref[row, q * C : q * C + C, :] = part
+def put_stack(ref, row, main, side, d, wide=False):
+    lane = lax.broadcasted_iota(jnp.int32, (C, BR), 1)
+    last = lane >= BR - d
+    first = lane < d
+    ref[row, 0:C, 0:BR] = pltpu.roll(jnp.where(last, side, main), d, 1)
+    ref[row, C : 2 * C, 0:BR] = main
+    ref[row, 2 * C : 3 * C, 0:BR] = pltpu.roll(jnp.where(first, side, main), BR - d, 1)
+    if wide:
+        ref[row, 0:C, BR : 2 * BR] = pltpu.roll(jnp.where(last, main, side), d, 1)
+        ref[row, C : 2 * C, BR : 2 * BR] = side
+        ref[row, 2 * C : 3 * C, BR : 2 * BR] = pltpu.roll(jnp.where(first, main, side), BR - d, 1)
 
 
 def taps(ref, row, d):
@@ -123,7 +123,7 @@
             def _():
                 dst[...] = jnp.zeros(dst.shape, BF)
 
-    def start(self):
+    def pack_sides(self):
         h, per = self.h, self.per
         group = lax.broadcasted_iota(jnp.int32, (C, BR), 1) // h
 
@@ -132,13 +132,16 @@
             high = jnp.zeros((C, BR), BF)
             for j in range(per):
                 v = self.own[t * per + j]
-                low = jnp.where(group == j, pltpu.roll(v, j * h, 1), low)
-                high = jnp.where(group == j, pltpu.roll(v, (j * h + h) % BR, 1), high)
+                turned = pltpu.roll(v, j * h, 1) if j else v
+                low = jnp.where(group == j, turned, low)
+                high = jnp.where(group == (j - 1) % per, turned, high)
             self.pack[0, t] = low
             self.pack[1, t] = high
             return carry
 
         lax.fori_loop(0, self.count, pack, 0)
+
+    def start(self):
         for k, piece in enumerate(self.pieces()):
 
             @pl.when(self.place.inside(piece[0], piece[1]))
@@ -161,7 +164,7 @@
 
     def build(self, ref, d):
         h, per, e = self.h, self.per, self.edge
-        lane = lax.broadcasted_iota(jnp.int32, (C, BR), 1)
+        group = lax.broadcasted_iota(jnp.int32, (C, BR), 1) // h
 
         def segment(main, first, pack, j0, nj, packs):
             def step(t, carry):
@@ -171,16 +174,13 @@
                     j = j0 + u
                     row = t * nj + u
                     side = jnp.where(
-                        lane < h,
-                        pltpu.roll(low, (BR - j * h) % BR, 1),
-                        jnp.where(
-                            lane >= BR - h,
-                            pltpu.roll(high, (2 * BR - h - j * h) % BR, 1),
-                            jnp.zeros((C, BR), BF),
-                        ),
+                        group == j,
+                        low,
+                        jnp.where(group == (j - 1) % per, high, jnp.zeros((C, BR), BF)),
                     )
-                    v = jnp.concatenate([main[row], side], axis=1)
-                    put_stack(ref, first + row, v, d, 2 * BR)
+                    if j:
+                        side = pltpu.roll(side, BR - j * h, 1)
+                    put_stack(ref, first + row, main[row], side, d, True)
                 return carry
 
             lax.fori_loop(0, packs, step, 0)
@@ -214,10 +214,15 @@
         ]
 
     def relay_of(self, ri, cq, s, q):
-        return 2 * (q // 2) + lax.rem(ri, 2), 4 * (2 * (cq // 2) + lax.rem(q, 2)) + s
+        other = lax.rem(s + 2 * lax.rem(q + cq, 2), 4)
+        return 2 * (q // 2) + lax.rem(ri, 2), 4 * (2 * (cq // 2) + lax.rem(q, 2)) + other
 
     def source(self, w):
-        return 2 * (w // 2) + lax.rem(self.ri, 2), 2 * (self.cq // 2) + lax.rem(w, 2)
+        return (
+            2 * (w // 2) + lax.rem(self.ri, 2),
+            2 * (self.cq // 2) + lax.rem(w, 2),
+            lax.rem(self.s + 2 * lax.rem(w + self.cq, 2), 4),
+        )
 
     def my_w(self):
         return 2 * (self.ri // 2) + lax.rem(self.cq, 2)
@@ -240,7 +245,7 @@
         return self.relay_of(self.ri, self.cq, self.s, q)
 
     def target2(self, w, k):
-        ri, cq = self.source(w)
+        ri, cq, _ = self.source(w)
         return cq, 4 * ri + k
 
     def is_self(self, device):
@@ -280,8 +285,9 @@
 
         def step(w, carry):
             self.arrived(self.first(0, w), self.send1.at[0])
+            slot = self.source(w)[2]
             for k in range(4):
-                self.go(self.second(w, k, self.s, mine), self.send2.at[w, k], self.target2(w, k))
+                self.go(self.second(w, k, slot, mine), self.send2.at[w, k], self.target2(w, k))
             return carry
 
         lax.fori_loop(0, self.n, step, 0)
@@ -312,8 +318,8 @@
 
     def greet(self, greet):
         def step(q, count):
-            ri, cq = self.source(q)
-            source = ri, 4 * cq + self.s
+            ri, cq, s = self.source(q)
+            source = ri, 4 * cq + s
 
             @pl.when(jnp.logical_not(self.is_self(source)))
             def _():
@@ -370,39 +376,126 @@
     return jnp.concatenate(groups, axis=1)
 
 
-def kernel_grad(padding, own, stacked, d, out, first):
-    padding[...] = jnp.zeros(padding.shape, BF)
-
+class Total:
+    def __init__(self, place, refs):
+        self.place = place
+        self.acc, self.r1, self.mine, self.r2, self.fin = refs[:5]
+        self.send1, self.recv1, self.send2, self.recv2, self.send3, self.recv3 = refs[5:]
+        self.owners = self.acc.shape[0]
+        self.n1 = place.ncol // 2
+        self.n2 = 2 * place.nrow
+        self.a = lax.rem(place.ci, self.n1)
+        self.half = place.ci // self.n1
+        self.m = place.ri * 2 + self.half
+        self.owner = self.a < self.owners
+
+    @staticmethod
+    def scratch(n1, n2, owners, count):
+        block = (count, 3 * C // owners, BR)
+        vmem = pltpu.VMEM
+        return [
+            vmem((owners,) + block, F32),
+            vmem((n1,) + block, F32),
+            vmem(block, F32),
+            vmem((n2,) + block, F32),
+            vmem((owners,) + block, F32),
+        ] + [pltpu.SemaphoreType.DMA((n,)) for n in (owners, n1, n2, n2, n1, owners)]
+
+    def group1(self, b):
+        return self.place.ri, self.half * self.n1 + b
+
+    def group2(self, m):
+        return m // 2, lax.rem(m, 2) * self.n1 + self.a
+
+    def others(self, count, me, body):
+        def step(b, carry):
+            @pl.when(b != me)
+            def _():
+                body(b)
+
+            return carry
+
+        lax.fori_loop(0, count, step, 0)
+
+    def share(self, src, dst, send, recv, device):
+        return pltpu.make_async_remote_copy(
+            src_ref=src, dst_ref=dst, send_sem=send, recv_sem=recv, device_id=device, device_id_type=MESH
+        )
+
+    def scatter(self, b, slot):
+        return self.share(
+            self.acc.at[b], self.r1.at[slot], self.send1.at[b], self.recv1.at[slot], self.group1(b)
+        )
+
+    def spread(self, m, slot):
+        return self.share(
+            self.mine, self.r2.at[slot], self.send2.at[m], self.recv2.at[slot], self.group2(m)
+        )
+
+    def gather(self, b, src, slot):
+        return self.share(
+            self.fin.at[src], self.fin.at[slot], self.send3.at[b], self.recv3.at[slot], self.group1(b)
+        )
+
+    def start1(self):
+        self.others(self.owners, self.a, lambda b: self.scatter(b, self.a).start())
+
+    def start2(self):
+        @pl.when(self.owner)
+        def _():
+            self.r1[self.a] = self.acc[self.a]
+            self.others(self.n1, self.a, lambda b: self.scatter(0, b).wait_recv())
+            self.mine[...] = sum(self.r1[b] for b in range(self.n1))
+            self.others(self.n2, self.m, lambda m: self.spread(m, self.m).start())
+            self.r2[self.m] = self.mine[...]
+
+    def start3(self):
+        @pl.when(self.owner)
+        def _():
+            self.others(self.n2, self.m, lambda m: self.spread(m, m).wait_recv())
+            self.fin[self.a] = sum(self.r2[m] for m in range(self.n2))
+            self.others(self.n1, self.a, lambda b: self.gather(b, self.a, self.a).start())
+
+    def finish(self):
+        self.others(self.owners, self.a, lambda b: self.gather(0, 0, b).wait_recv())
+
+    def drain(self):
+        self.others(self.owners, self.a, lambda b: self.scatter(b, 0).wait_send())
+
+        @pl.when(self.owner)
+        def _():
+            self.others(self.n2, self.m, lambda m: self.spread(m, 0).wait_send())
+            self.others(self.n1, self.a, lambda b: self.gather(b, self.a, 0).wait_send())
+
+
+def kernel_grad(padding, own, stacked, d, out, which):
     def fill(k):
         padding[k + 2 * d] = own(k)
 
-    rows(BC, fill)
-
-    def step(t, acc):
+    rows(BC, fill, 16)
+    total = jnp.zeros((3 * C, 3 * C), F32)
+    for t in range((BC + 2 * d) // 8):
         left = []
         right = []
-        for u in range(8):
-            k = t * 8 + u
+        for k in range(t * 8, t * 8 + 8):
             left.append(
                 jnp.concatenate([padding[k + 2 * d], padding[k + d], padding[k]], axis=0)
             )
             right.append(stacked[k, :, 0:BR])
-        return acc + lax.dot_general(
+        total = total + lax.dot_general(
             jnp.concatenate(left, axis=1),
             jnp.concatenate(right, axis=1),
             (((1,), (1,)), ((), ())),
             preferred_element_type=F32,
         )
-
-    total = lax.fori_loop(0, (BC + 2 * d) // 8, step, jnp.zeros((3 * C, 3 * C), F32))
-    per = out.shape[1]
+    per = out.shape[2]
     for t in range(3 * C // per):
-        out[first * (3 * C) // per + t, :, 0 : 3 * C] = total[t * per : t * per + per]
+        out[t, which, :, 0 : 3 * C] = total[t * per : t * per + per]
 
 
 def main_kernel(nrow, ncol, *refs):
-    (x_ref, g_ref, fa, fb, sa, sb, dec, g0, kg) = refs[:9]
-    rest = list(refs[9:])
+    inputs, (dec_out, g0_out, early_out, late_out) = refs[:6], refs[6:10]
+    rest = list(refs[10:])
 
     def take(n):
         out = rest[:n]
@@ -415,27 +508,26 @@
     halo_s2 = Halo(16, place, take(7))
     halo_z = Halo(16, place, take(7))
     halo_s1 = Halo(8, place, take(7))
+    halos = (halo_x, halo_s2, halo_z, halo_s1)
     mir_g = Mirror(place, take(7))
     mir_y = Mirror(place, take(7))
+    early = Total(place, take(11))
+    late = Total(place, take(11))
+    held = take(6)
+    x_ref, g_ref, fa, fb, sa, sb = held
+    in_sem, out_sem = take(2)
     (wa1, wb1, wa2, wb2, wb2t, tb2, ta2, ta2t, tb1, ta1) = take(10)
-    (xc1, hc1, slope1, xc2, sc2, hg2, hc2, hc2t, ec2, ec2t, sc1, ec1, y1, e2own, e1own) = take(15)
-    (pad, acc, r1, mine, r2, fin, s1_send, s1_recv, s2_send, s2_recv, s3_send, s3_recv) = take(12)
-    halos = (halo_x, halo_s2, halo_z, halo_s1)
-
-    n1 = ncol // 2
-    n2 = 2 * nrow
-    a = lax.rem(ci, n1)
-    half = ci // n1
-    me2 = ri * 2 + half
-
-    def group1(b):
-        return ri, half * n1 + b
-
-    def group2(m):
-        return m // 2, lax.rem(m, 2) * n1 + a
+    (xc1, hc1, slope1, xc2, sc2, hg2, hc2, hc2t, ec2, ec2t, sc1, ec1, y1, dec, g0) = take(15)
+    pad1, pad2 = take(2)
+
+    loads = [
+        pltpu.make_async_copy(src, dst, in_sem.at[k]) for k, (src, dst) in enumerate(zip(inputs, held))
+    ]
+    for load in loads:
+        load.start()
 
     barrier = pltpu.get_barrier_semaphore()
-    expected = jnp.int32(n1 + n2 - 2)
+    expected = jnp.int32(early.n1 + early.n2 - 2)
 
     def greet(row, col):
         pl.semaphore_signal(barrier, inc=1, device_id=(row, col), device_id_type=MESH)
@@ -451,40 +543,27 @@
                     greet(ri + dr, ci + dc)
 
     expected = expected + mir_g.greet(greet)
-
-    def greet1(b, carry):
-        @pl.when(b != a)
-        def _():
-            greet(*group1(b))
-
-        return carry
-
-    def greet2(m, carry):
-        @pl.when(m != me2)
-        def _():
-            greet(*group2(m))
-
-        return carry
-
-    lax.fori_loop(0, n1, greet1, 0)
-    lax.fori_loop(0, n2, greet2, 0)
+    early.others(early.n1, early.a, lambda b: greet(*early.group1(b)))
+    early.others(early.n2, early.m, lambda m: greet(*early.group2(m)))
 
     order = permutation(False)
+    loads[0].wait()
     flat = x_ref[...].reshape(C * BC, BR)
     halo_x.own[...] = interleave(
         [dot(order, flat[256 * t : 256 * t + 256]).reshape(BC, 8, BR) for t in range(4)]
     ).astype(BF)
+    halo_x.pack_sides()
+    for load in loads[1:]:
+        load.wait()
     gflat = g_ref[...].reshape(C * BC, BR)
     for j in range(8):
         mir_g.out[j] = gflat[j * BR : j * BR + BR].T
-    for halo in halos:
-        halo.fill_edges()
+    fill_matrix(wa1, 0, fa, False, False)
+    fill_matrix(wb1, 0, fb, False, False)
     pl.semaphore_wait(barrier, expected)
     halo_x.start()
     mir_g.start()
 
-    fill_matrix(wa1, 0, fa, False, False)
-    fill_matrix(wb1, 0, fb, False, False)
     fill_matrix(wa2, 0, sa, False, False)
     fill_matrix(wa2, C, sa, False, True)
     fill_matrix(wb2, 0, sb, False, False)
@@ -495,16 +574,22 @@
     fill_matrix(ta2t, 0, sa, True, True)
     fill_matrix(tb1, 0, fb, True, False)
     fill_matrix(ta1, 0, fa, True, False)
-
-    lane = lax.broadcasted_iota(jnp.int32, (C, 2 * BR), 1)
-    first_lane = jnp.where(ri < nrow - 1, BR, BR + 64)
-    last_lane = jnp.where(ri > 0, 2 * BR, BR + 64)
-    lane_ok = (lane < BR) | ((lane >= first_lane) & (lane < last_lane))
-
-    def on_map(row, v):
-        bin_index = ci * BC + row
+    for halo in halos:
+        halo.fill_edges()
+    for ref in (pad1, pad2, early.acc, late.acc):
+        ref[...] = jnp.zeros(ref.shape, ref.dtype)
+
+    lane = lax.broadcasted_iota(jnp.int32, (C, BR), 1)
+    first_lane = jnp.where(ri < nrow - 1, 0, 64)
+    last_lane = jnp.where(ri > 0, BR, 64)
+    side_ok = (lane >= first_lane) & (lane < last_lane)
+
+    def put_field(ref, k, d, v):
+        bin_index = ci * BC + k - d
         ok = (bin_index >= 0) & (bin_index < ncol * BC)
-        return jnp.where(lane_ok & ok, v, 0.0)
+        main = jnp.where(ok, v[:, :BR], 0.0).astype(BF)
+        side = jnp.where(side_ok & ok, v[:, BR:], 0.0).astype(BF)
+        put_stack(ref, k, main, side, d)
 
     d = DILATE_ONE
     halo_x.wait()
@@ -514,15 +599,15 @@
         pre = dot(wa1[...], taps(xc1, k, d))
         sig = jax.nn.sigmoid(pre)
         slope1[k] = sig * (1.0 + pre * (1.0 - sig))
-        put_stack(hc1, k, on_map(k - d, pre * sig).astype(BF), d, BR)
-
-    rows(BC + 2 * d, hidden1)
+        put_field(hc1, k, d, pre * sig)
+
+    rows(BC + 2 * d, hidden1, 10)
     mir_g.forward()
 
     def outer1(k):
         y1[k] = (halo_x.own[k].astype(F32) + dot(wb1[...], taps(hc1, k, d))).astype(BF)
 
-    rows(BC, outer1)
+    rows(BC, outer1, 16)
 
     back = permutation(True)
     for t in range(4):
@@ -543,8 +628,11 @@
         mean = ((here.astype(F32) + mirrored.astype(F32)) * 0.5).astype(BF)
         parts.append(dot(order, mean).reshape(BC, 8, BR))
     halo_s2.own[...] = interleave(parts).astype(BF)
+    halo_s2.pack_sides()
     halo_s2.start()
     mir_y.forward()
+    halo_s2.wait()
+    halo_s2.build(sc2, DILATE_TWO)
 
     mir_y.wait()
     turned = mir_y.fetch()
@@ -555,16 +643,15 @@
         )
         parts.append(dot(order, mirrored).reshape(BC, 8, BR))
     halo_z.own[...] = ((y1[...].astype(F32) + interleave(parts)) * 0.5).astype(BF)
+    halo_z.pack_sides()
     halo_z.start()
 
     d = DILATE_TWO
-    halo_s2.wait()
-    halo_s2.build(sc2, d)
 
     def cotangent2(k):
         hg2[k] = dot(tb2[...], taps(sc2, k, d))
 
-    rows(BC + 2 * d, cotangent2)
+    rows(BC + 2 * d, cotangent2, 16)
     halo_z.wait()
     halo_z.build(xc2, d)
 
@@ -573,12 +660,12 @@
         sig = jax.nn.sigmoid(pre)
         hid = pre * sig
         grad = hg2[k] * (sig * (1.0 + pre * (1.0 - sig)))
-        put_stack(hc2, k, on_map(k - d, hid[:C]).astype(BF), d, BR)
-        put_stack(hc2t, k, on_map(k - d, hid[C:]).astype(BF), d, BR)
-        put_stack(ec2, k, on_map(k - d, grad[:C]).astype(BF), d, BR)
-        put_stack(ec2t, k, on_map(k - d, grad[C:]).astype(BF), d, BR)
-
-    rows(BC + 2 * d, hidden2, 4)
+        put_field(hc2, k, d, hid[:C])
+        put_field(hc2t, k, d, hid[C:])
+        put_field(ec2, k, d, grad[:C])
+        put_field(ec2t, k, d, grad[C:])
+
+    rows(BC + 2 * d, hidden2, 8)
 
     def upstream1(k):
         base = halo_s2.own[k].astype(F32)
@@ -586,105 +673,98 @@
         two = (base + dot(ta2t[...], taps(ec2t, k, d))).astype(BF)
         halo_s1.own[k] = ((one.astype(F32) + two.astype(F32)) * 0.5).astype(BF)
 
-    rows(BC, upstream1)
+    rows(BC, upstream1, 16)
+    halo_s1.pack_sides()
     halo_s1.start()
+    kernel_grad(pad2, lambda k: halo_s2.own[k], hc2, d, early.acc, 2)
+    kernel_grad(
+        pad2, lambda k: ec2[k + DILATE_TWO, C : 2 * C, :], xc2.at[d : d + BC + 2 * d], d, early.acc, 1
+    )
+
+    d = DILATE_ONE
+    kernel_grad(pad1, lambda k: halo_s1.own[k], hc1, d, early.acc, 0)
+    early.start1()
+    halo_s1.wait()
+    halo_s1.build(sc1, d)
+
+    def cotangent1(k):
+        put_field(ec1, k, d, dot(tb1[...], taps(sc1, k, d)) * slope1[k])
+
+    rows(BC + 2 * d, cotangent1, 10)
+    kernel_grad(
+        pad1, lambda k: ec1[k + DILATE_ONE, C : 2 * C, :], xc1.at[d : d + BC + 2 * d], d, late.acc, 0
+    )
+    late.start1()
+    early.start2()
+
+    def upstream0(k):
+        g0[k] = (halo_s1.own[k].astype(F32) + dot(ta1[...], taps(ec1, k, d))).astype(BF)
+
+    rows(BC, upstream0, 16)
+    g0_copy = pltpu.make_async_copy(g0, g0_out, out_sem.at[0])
+    g0_copy.start()
+    late.start2()
 
     def outer2(k):
         base = halo_z.own[k].astype(F32)
-        one = (base + dot(wb2[...], taps(hc2, k, d))).astype(BF)
-        two = (base + dot(wb2t[...], taps(hc2t, k, d))).astype(BF)
+        one = (base + dot(wb2[...], taps(hc2, k, DILATE_TWO))).astype(BF)
+        two = (base + dot(wb2t[...], taps(hc2t, k, DILATE_TWO))).astype(BF)
         dec[k] = ((one.astype(F32) + two.astype(F32)) * 0.5).astype(BF)
 
-    rows(BC, outer2)
-    acc[...] = jnp.zeros(acc.shape, F32)
-    kernel_grad(pad.at[0 : BC + 4 * d], lambda k: halo_s2.own[k], hc2, d, acc, 3)
-    kernel_grad(
-        pad.at[0 : BC + 4 * d], lambda k: ec2[k + DILATE_TWO, C : 2 * C, :], xc2.at[d : d + BC + 2 * d], d, acc, 2
-    )
-
-    d = DILATE_ONE
-    kernel_grad(pad.at[0 : BC + 4 * d], lambda k: halo_s1.own[k], hc1, d, acc, 1)
-    halo_s1.wait()
-    halo_s1.build(sc1, d)
-
-    def cotangent1(k):
-        grad = dot(tb1[...], taps(sc1, k, d)) * slope1[k]
-        put_stack(ec1, k, on_map(k - d, grad).astype(BF), d, BR)
-
-    rows(BC + 2 * d, cotangent1)
-    kernel_grad(
-        pad.at[0 : BC + 4 * d], lambda k: ec1[k + DILATE_ONE, C : 2 * C, :], xc1.at[d : d + BC + 2 * d], d, acc, 0
-    )
-
-    def share(src, dst, send, recv, slot, device):
-        return pltpu.make_async_remote_copy(
-            src_ref=src, dst_ref=dst, send_sem=send, recv_sem=recv, device_id=device, device_id_type=MESH
-        )
-
-    def others(count, me, body):
-        def step(b, carry):
-            @pl.when(b != me)
-            def _():
-                body(b)
-
-            return carry
-
-        lax.fori_loop(0, count, step, 0)
-
-    def scatter(b, slot):
-        return share(acc.at[b], r1.at[slot], s1_send.at[b], s1_recv.at[slot], slot, group1(b))
-
-    def spread(m, slot):
-        return share(mine, r2.at[slot], s2_send.at[m], s2_recv.at[slot], slot, group2(m))
-
-    def gather(b, slot):
-        return share(fin.at[a], fin.at[slot], s3_send.at[b], s3_recv.at[slot], slot, group1(b))
-
-    others(n1, a, lambda b: scatter(b, a).start())
-
-    def upstream0(k):
-        g0[k] = (halo_s1.own[k].astype(F32) + dot(ta1[...], taps(ec1, k, d))).astype(BF)
-
-    rows(BC, upstream0)
-    r1[a] = acc[a]
-    others(n1, a, lambda b: scatter(b, b).wait_recv())
-    mine[...] = lax.fori_loop(1, n1, lambda b, total: total + r1[b], r1[0])
-    others(n2, me2, lambda m: spread(m, me2).start())
-    r2[me2] = mine[...]
-    others(n2, me2, lambda m: spread(m, m).wait_recv())
-    fin[a] = lax.fori_loop(1, n2, lambda m, total: total + r2[m], r2[0])
-    others(n1, a, lambda b: gather(b, a).start())
+    rows(BC, outer2, 16)
+    dec_copy = pltpu.make_async_copy(dec, dec_out, out_sem.at[1])
+    dec_copy.start()
+    early.start3()
+    late.start3()
     for halo in halos:
         halo.drain()
     mir_g.drain()
     mir_y.drain()
-    others(n1, a, lambda b: scatter(b, a).wait_send())
-    others(n2, me2, lambda m: spread(m, me2).wait_send())
-    others(n1, a, lambda b: gather(b, b).wait_recv())
-    others(n1, a, lambda b: gather(b, a).wait_send())
-    kg[...] = fin[...].reshape(kg.shape)
-
-
-def finish_kernel(dec, g0, kg, out_dec, out_g0, out_a1, out_b1, out_a2, out_b2):
+    early.finish()
+    early_copy = pltpu.make_async_copy(early.fin, early_out, out_sem.at[2])
+    early_copy.start()
+    late.finish()
+    late_copy = pltpu.make_async_copy(late.fin, late_out, out_sem.at[3])
+    late_copy.start()
+    early.drain()
+    late.drain()
+    for copy in (g0_copy, dec_copy, early_copy, late_copy):
+        copy.wait()
+
+
+def finish_kernel(dec_in, g0_in, early_in, late_in, out_dec, out_g0, out_a1, out_b1, out_a2, out_b2, *rest):
+    held, sems = rest[:4], rest[4]
+    loads = [
+        pltpu.make_async_copy(src, dst, sems.at[k])
+        for k, (src, dst) in enumerate(zip((dec_in, g0_in, early_in, late_in), held))
+    ]
+    for load in loads:
+        load.start()
     back = permutation(True)
-    for src, dst in ((dec, out_dec), (g0, out_g0)):
+    for load, src, dst in zip(loads, held, (out_dec, out_g0)):
+        load.wait()
         whole = src[...].astype(F32)
         for t in range(4):
             part = whole[:, 8 * t : 8 * t + 8, :].reshape(256, BR).astype(BF)
             dst[8 * t : 8 * t + 8] = dot(back, part).astype(BF).reshape(8, BC, BR)
-    for k, dst in enumerate((out_a1, out_b1, out_a2, out_b2)):
+    early, late = held[2:]
+    loads[2].wait()
+    loads[3].wait()
+    owners = early.shape[0]
+    for src, which, dst in ((late, 0, out_a1), (early, 0, out_b1), (early, 1, out_a2), (early, 2, out_b2)):
+        band = src[:, which].reshape(3 * C, BR)
         for p in range(3):
-            band = kg[(3 * k + p) * C : (3 * k + p) * C + C, :]
             for q in range(3):
-                dst[p, q] = band[:, q * C : q * C + C]
-
-
-def per_device(nrow, ncol, pair_map, out_grad, first_a, first_b, second_a, second_b):
+                dst[p, q] = band[p * C : p * C + C, q * C : q * C + C]
+
+
+def per_device(nrow, ncol, *arrays):
     n1 = ncol // 2
     n2 = 2 * nrow
-    per = 12 * C // n1
+    owners = 12 if n1 >= 12 else 4
     wide = BC + 16
     vmem = pltpu.VMEM
+    grad_shapes = [(owners, count, 3 * C // owners, BR) for count in (3, 1)]
     scratch = (
         Halo.scratch(8)
         + Halo.scratch(16)
@@ -692,6 +772,11 @@
         + Halo.scratch(8)
         + Mirror.scratch(nrow)
         + Mirror.scratch(nrow)
+        + Total.scratch(n1, n2, owners, 3)
+        + Total.scratch(n1, n2, owners, 1)
+        + [vmem((C, BC, BR), BF)] * 2
+        + [vmem((3, 3, C, C), BF)] * 4
+        + [pltpu.SemaphoreType.DMA((6,)), pltpu.SemaphoreType.DMA((4,))]
         + [vmem((m, 9 * C), BF) for m in (C, C, 2 * C, C, C, 2 * C, C, C, C, C)]
         + [
             vmem((BC + 16, 3 * C, 2 * BR), BF),
@@ -707,51 +792,39 @@
             vmem((BC + 16, 3 * C, 2 * BR), BF),
             vmem((BC + 8, 3 * C, BR), BF),
             vmem((BC, C, BR), BF),
-            vmem((8, BR), F32),
-            vmem((8, BR), F32),
+            vmem((BC, C, BR), BF),
+            vmem((BC, C, BR), BF),
+            vmem((BC + 16, C, BR), BF),
+            vmem((BC + 32, C, BR), BF),
         ]
-        + [
-            vmem((BC + 32, C, BR), BF),
-            vmem((n1, per, BR), F32),
-            vmem((n1, per, BR), F32),
-            vmem((per, BR), F32),
-            vmem((n2, per, BR), F32),
-            vmem((n1, per, BR), F32),
-        ]
-        + [pltpu.SemaphoreType.DMA((n,)) for n in (n1, n1, n2, n2, n1, n1)]
     )
     whole = pl.BlockSpec(memory_space=pltpu.VMEM)
-    dec, g0, kg = pl.pallas_call(
+    anywhere = pl.BlockSpec(memory_space=pl.ANY)
+    by_bin = jax.ShapeDtypeStruct((BC, C, BR), BF)
+    results = pl.pallas_call(
         functools.partial(main_kernel, nrow, ncol),
-        out_shape=[
-            jax.ShapeDtypeStruct((BC, C, BR), BF),
-            jax.ShapeDtypeStruct((BC, C, BR), BF),
-            jax.ShapeDtypeStruct((12 * C, BR), F32),
-        ],
-        in_specs=[whole] * 6,
-        out_specs=[whole] * 3,
+        out_shape=[by_bin, by_bin] + [jax.ShapeDtypeStruct(shape, F32) for shape in grad_shapes],
+        in_specs=[anywhere] * 6,
+        out_specs=[anywhere] * 4,
         scratch_shapes=scratch,
         compiler_params=pltpu.CompilerParams(
             collective_id=0, has_side_effects=True, vmem_limit_bytes=56 << 20
         ),
         name="blocks",
-    )(pair_map, out_grad, first_a, first_b, second_a, second_b)
+    )(*arrays)
     small = jax.ShapeDtypeStruct((3, 3, C, C), F32)
+    field = jax.ShapeDtypeStruct((C, BC, BR), BF)
     return pl.pallas_call(
         finish_kernel,
-        out_shape=[
-            jax.ShapeDtypeStruct((C, BC, BR), BF),
-            jax.ShapeDtypeStruct((C, BC, BR), BF),
-            small,
-            small,
-            small,
-            small,
-        ],
-        in_specs=[whole] * 3,
+        out_shape=[field, field, small, small, small, small],
+        in_specs=[anywhere] * 4,
         out_specs=[whole] * 6,
-        compiler_params=pltpu.CompilerParams(vmem_limit_bytes=24 << 20),
+        scratch_shapes=[vmem((BC, C, BR), BF)] * 2
+        + [vmem(shape, F32) for shape in grad_shapes]
+        + [pltpu.SemaphoreType.DMA((4,))],
+        compiler_params=pltpu.CompilerParams(vmem_limit_bytes=56 << 20),
         name="finish",
-    )(dec, g0, kg)
+    )(*results)
 
 
 def solution(mesh):

time: 108 us -> 101 us (0.935)
  Pallas kernels: 104 us -> 99.8 us
  local copies, waits for them, and re-layouts: 2.82 us -> 0 us
    pallas_call x2, Pallas kernels: 104 us -> 99.8 us  [the longest x1 97.3 us: per_device(): pl.pallas_call(functools.partial(main_kernel, nrow, ncol), out_shape=[by_...]
    unnamed x6 -> x0, local copies, waits for them, and re-layouts: 2.82 us -> none
where the time goes in v3:
time: 101 us; the launch traced here: 100 us
  Pallas kernels  99.8 us (99%)
    pallas_call x1, Pallas kernels, per_device(): pl.pallas_call(functools.partial(main_kernel, nrow, ncol), out_shape=[by_...  97.3 us
    pallas_call x1, Pallas kernels, per_device(): pl.pallas_call(finish_kernel, out_shape=[field, field, small, small, smal...  2.54 us

profile of v3, /device:TPU:1, one launch (start us, length us, event | category | flops | bytes accessed | tf_op | source)
XLA Modules:
  0.0 100.4 jit_solution(882288382507828891)
XLA Ops:
  0.6 97.3 %blocks.1 = (bf16[32,32,128]{2,1,0:T(8,128)(2,1)}, bf16[32,32,128]{2,1,0:T(8,128)(2,1)}, f32[12,3,8,128]{3,2,1,0:T(8,128)}, f32[12,1,8,128]{3,2,1,0:T(8,128)}) custom-call(bf16[32,32,128]{2,1,0:T(8,128)(2,1)} %refs_0_.1, bf16[32,32,128]{2,1,0:T(8,128)(2,1)} %refs_1_.1, bf16[3,3,32,32]{3,2,1,0:T(8,128)(2,1)} %refs_2_.1, bf16[3,3,32,32]{3,2,1,0:T(8,128)(2,1)} %refs_3_.1, ...), custom_call_target="tpu_custom_call" | custom-call | tf_op jit(solution)/shard_map/blocks/pallas_call | solution.py:804
  97.9 2.5 %finish.1 = (bf16[32,32,128]{2,1,0:T(8,128)(2,1)}, bf16[32,32,128]{2,1,0:T(8,128)(2,1)}, f32[3,3,32,32]{3,2,1,0:T(8,128)}, f32[3,3,32,32]{3,2,1,0:T(8,128)}, f32...) custom-call(bf16[32,32,128]{2,1,0:T(8,128)(2,1)} %get-tuple-element.10.dec_in, ...), custom_call_target="tpu_custom_call" | custom-call | tf_op jit(solution)/shard_map/finish/pallas_call | solution.py:817

commit v4 on v3

--- a/solution.py
+++ b/solution.py
@@ -59,20 +59,32 @@
     return jnp.concatenate([ref[row], ref[row + d], ref[row + 2 * d]], axis=0)
 
 
-def rows(count, body, unroll=8):
+def rows(count, body, unroll=8, first=0):
     def step(t, carry):
         for u in range(unroll):
-            body(t * unroll + u)
+            body(first + t * unroll + u)
         return carry
 
     lax.fori_loop(0, count // unroll, step, 0)
+
+
+def outer_rows(body, unroll):
+    per = 16 // unroll
+
+    def step(t, carry):
+        for u in range(unroll):
+            body(t * unroll + (t // per) * 16 + u)
+        return carry
+
+    lax.fori_loop(0, 2 * per, step, 0)
 
 
 class Halo:
     names = ("own", "top", "bottom", "pack", "land", "send", "recv")
 
-    def __init__(self, width, place, refs):
+    def __init__(self, width, place, refs, by_way=False):
         self.h = width
+        self.by_way = by_way
         self.per = BR // width
         self.edge = 16 // self.per
         self.count = BC // self.per
@@ -94,7 +106,8 @@
 
     def pieces(self):
         e, n, h = self.edge, self.count, self.h
-        return (
+        out = []
+        for dr, dc, src, dst in (
             (0, -1, self.own.at[0:h], self.bottom),
             (0, 1, self.own.at[BC - h : BC], self.top),
             (-1, 0, self.pack.at[0], self.land.at[0, e : e + n]),
@@ -103,21 +116,62 @@
             (-1, 1, self.pack.at[0, n - e : n], self.land.at[0, 0:e]),
             (1, -1, self.pack.at[1, 0:e], self.land.at[1, e + n :]),
             (1, 1, self.pack.at[1, n - e : n], self.land.at[1, 0:e]),
-        )
+        ):
+            target = (self.place.ri + dr, self.place.ci + dc)
+            sends = self.place.inside(dr, dc)
+            if self.by_way and dr and dc:
+                side = 0 if dr < 0 else 1
+                src = self.land.at[side, e : 2 * e] if dc < 0 else self.land.at[side, n : e + n]
+                target = (self.place.ri, self.place.ci + dc)
+                sends = self.place.inside(-dr, dc)
+            out.append((dr, dc, src, dst, target, sends))
+        return out
 
     def copy(self, k, piece):
-        dr, dc, src, dst = piece
         return pltpu.make_async_remote_copy(
-            src_ref=src,
-            dst_ref=dst,
+            src_ref=piece[2],
+            dst_ref=piece[3],
             send_sem=self.send.at[k],
             recv_sem=self.recv.at[k],
-            device_id=(self.place.ri + dr, self.place.ci + dc),
+            device_id=piece[4],
             device_id_type=MESH,
         )
 
+    def launch(self, which):
+        for k, piece in enumerate(self.pieces()):
+            if k in which:
+
+                @pl.when(piece[5])
+                def _():
+                    self.copy(k, piece).start()
+
+    def accept(self, which):
+        for k, piece in enumerate(self.pieces()):
+            if k in which:
+
+                @pl.when(self.place.inside(-piece[0], -piece[1]))
+                def _():
+                    self.copy(k, piece).wait_recv()
+
+    def start(self):
+        self.launch((2, 3, 0, 1) if self.by_way else range(8))
+
+    def forward(self):
+        self.accept((2, 3))
+        self.launch((4, 5, 6, 7))
+
+    def wait(self):
+        self.accept((0, 1, 4, 5, 6, 7) if self.by_way else range(8))
+
+    def drain(self):
+        for k, piece in enumerate(self.pieces()):
+
+            @pl.when(piece[5])
+            def _():
+                self.copy(k, piece).wait_send()
+
     def fill_edges(self):
-        for dr, dc, src, dst in self.pieces():
+        for dr, dc, _, dst, _, _ in self.pieces():
 
             @pl.when(jnp.logical_not(self.place.inside(-dr, -dc)))
             def _():
@@ -141,30 +195,27 @@
 
         lax.fori_loop(0, self.count, pack, 0)
 
-    def start(self):
-        for k, piece in enumerate(self.pieces()):
-
-            @pl.when(self.place.inside(piece[0], piece[1]))
-            def _():
-                self.copy(k, piece).start()
-
-    def wait(self):
-        for k, piece in enumerate(self.pieces()):
-
-            @pl.when(self.place.inside(-piece[0], -piece[1]))
-            def _():
-                self.copy(k, piece).wait_recv()
-
-    def drain(self):
-        for k, piece in enumerate(self.pieces()):
-
-            @pl.when(self.place.inside(piece[0], piece[1]))
-            def _():
-                self.copy(k, piece).wait_send()
-
-    def build(self, ref, d):
+    def prepare(self, ref, d):
+        def own(k):
+            main = self.own[k]
+            ref[self.h + k, 0:C, 0:BR] = pltpu.roll(main, d, 1)
+            ref[self.h + k, C : 2 * C, 0:BR] = main
+            ref[self.h + k, 2 * C : 3 * C, 0:BR] = pltpu.roll(main, BR - d, 1)
+
+        rows(BC, own, 16)
+
+    def build(self, ref, d, inner=True, outer=True):
         h, per, e = self.h, self.per, self.edge
-        group = lax.broadcasted_iota(jnp.int32, (C, BR), 1) // h
+        lane = lax.broadcasted_iota(jnp.int32, (C, BR), 1)
+        group = lane // h
+
+        def complete(row, side):
+            ref[row, C : 2 * C, BR : 2 * BR] = side
+            for q, shift, edge in ((0, d, lane < d), (2, BR - d, lane >= BR - d)):
+                there = ref[row, q * C : q * C + C, 0:BR]
+                turned = pltpu.roll(side, shift, 1)
+                ref[row, q * C : q * C + C, 0:BR] = jnp.where(edge, turned, there)
+                ref[row, q * C : q * C + C, BR : 2 * BR] = jnp.where(edge, there, turned)
 
         def segment(main, first, pack, j0, nj, packs):
             def step(t, carry):
@@ -180,15 +231,20 @@
                     )
                     if j:
                         side = pltpu.roll(side, BR - j * h, 1)
-                    put_stack(ref, first + row, main[row], side, d, True)
+                    if main is self.own:
+                        complete(first + row, side)
+                    else:
+                        put_stack(ref, first + row, main[row], side, d, True)
                 return carry
 
             lax.fori_loop(0, packs, step, 0)
 
         nj = min(per, h)
-        segment(self.top, 0, 0, per - nj, nj, h // nj)
-        segment(self.own, h, e, 0, per, BC // per)
-        segment(self.bottom, h + BC, e + BC // per, 0, nj, h // nj)
+        if inner:
+            segment(self.own, h, e, 0, per, BC // per)
+        if outer:
+            segment(self.top, 0, 0, per - nj, nj, h // nj)
+            segment(self.bottom, h + BC, e + BC // per, 0, nj, h // nj)
 
 
 class Mirror:
@@ -505,8 +561,8 @@
     place = Place(nrow, ncol)
     ri, ci = place.ri, place.ci
     halo_x = Halo(8, place, take(7))
-    halo_s2 = Halo(16, place, take(7))
-    halo_z = Halo(16, place, take(7))
+    halo_s2 = Halo(16, place, take(7), True)
+    halo_z = Halo(16, place, take(7), True)
     halo_s1 = Halo(8, place, take(7))
     halos = (halo_x, halo_s2, halo_z, halo_s1)
     mir_g = Mirror(place, take(7))
@@ -518,7 +574,7 @@
     in_sem, out_sem = take(2)
     (wa1, wb1, wa2, wb2, wb2t, tb2, ta2, ta2t, tb1, ta1) = take(10)
     (xc1, hc1, slope1, xc2, sc2, hg2, hc2, hc2t, ec2, ec2t, sc1, ec1, y1, dec, g0) = take(15)
-    pad1, pad2 = take(2)
+    pad1, pad2, dec_nat, g0_nat = take(4)
 
     loads = [
         pltpu.make_async_copy(src, dst, in_sem.at[k]) for k, (src, dst) in enumerate(zip(inputs, held))
@@ -592,7 +648,9 @@
         put_stack(ref, k, main, side, d)
 
     d = DILATE_ONE
+    halo_x.prepare(xc1, d)
     halo_x.wait()
+    mir_g.forward()
     halo_x.build(xc1, d)
 
     def hidden1(k):
@@ -602,7 +660,6 @@
         put_field(hc1, k, d, pre * sig)
 
     rows(BC + 2 * d, hidden1, 10)
-    mir_g.forward()
 
     def outer1(k):
         y1[k] = (halo_x.own[k].astype(F32) + dot(wb1[...], taps(hc1, k, d))).astype(BF)
@@ -616,6 +673,7 @@
         for j in range(2):
             mir_y.out[2 * t + j] = natural[j * BR : j * BR + BR].T.astype(BF)
     mir_y.start()
+    mir_y.forward()
 
     mir_g.wait()
     turned = mir_g.fetch()
@@ -630,9 +688,9 @@
     halo_s2.own[...] = interleave(parts).astype(BF)
     halo_s2.pack_sides()
     halo_s2.start()
-    mir_y.forward()
-    halo_s2.wait()
-    halo_s2.build(sc2, DILATE_TWO)
+    halo_s2.prepare(sc2, DILATE_TWO)
+    halo_s2.forward()
+    halo_s2.build(sc2, DILATE_TWO, outer=False)
 
     mir_y.wait()
     turned = mir_y.fetch()
@@ -645,27 +703,32 @@
     halo_z.own[...] = ((y1[...].astype(F32) + interleave(parts)) * 0.5).astype(BF)
     halo_z.pack_sides()
     halo_z.start()
+    halo_z.prepare(xc2, DILATE_TWO)
 
     d = DILATE_TWO
 
     def cotangent2(k):
         hg2[k] = dot(tb2[...], taps(sc2, k, d))
 
+    halo_s2.wait()
+    halo_s2.build(sc2, d, inner=False)
     rows(BC + 2 * d, cotangent2, 16)
-    halo_z.wait()
-    halo_z.build(xc2, d)
+    halo_z.forward()
+    halo_z.build(xc2, d, outer=False)
 
     def hidden2(k):
         pre = dot(wa2[...], taps(xc2, k, d))
         sig = jax.nn.sigmoid(pre)
         hid = pre * sig
         grad = hg2[k] * (sig * (1.0 + pre * (1.0 - sig)))
-        put_field(hc2, k, d, hid[:C])
-        put_field(hc2t, k, d, hid[C:])
+        hg2[k] = hid
         put_field(ec2, k, d, grad[:C])
         put_field(ec2t, k, d, grad[C:])
 
-    rows(BC + 2 * d, hidden2, 8)
+    rows(16, hidden2, 8, 16)
+    halo_z.wait()
+    halo_z.build(xc2, d, inner=False)
+    outer_rows(hidden2, 8)
 
     def upstream1(k):
         base = halo_s2.own[k].astype(F32)
@@ -676,6 +739,12 @@
     rows(BC, upstream1, 16)
     halo_s1.pack_sides()
     halo_s1.start()
+    halo_s1.prepare(sc1, DILATE_ONE)
+
+    def place2(k):
+        put_field(hc2, k, DILATE_TWO, hg2[k, :C, :])
+
+    rows(BC + 2 * d, place2)
     kernel_grad(pad2, lambda k: halo_s2.own[k], hc2, d, early.acc, 2)
     kernel_grad(
         pad2, lambda k: ec2[k + DILATE_TWO, C : 2 * C, :], xc2.at[d : d + BC + 2 * d], d, early.acc, 1
@@ -697,13 +766,24 @@
     late.start1()
     early.start2()
 
+    def by_channel(src, dst):
+        for t in range(4):
+            part = src[:, 8 * t : 8 * t + 8, :].reshape(256, BR)
+            dst[8 * t : 8 * t + 8] = dot(back, part).astype(BF).reshape(8, BC, BR)
+
     def upstream0(k):
         g0[k] = (halo_s1.own[k].astype(F32) + dot(ta1[...], taps(ec1, k, d))).astype(BF)
 
     rows(BC, upstream0, 16)
-    g0_copy = pltpu.make_async_copy(g0, g0_out, out_sem.at[0])
+    by_channel(g0, g0_nat)
+    g0_copy = pltpu.make_async_copy(g0_nat, g0_out, out_sem.at[0])
     g0_copy.start()
     late.start2()
+
+    def place2t(k):
+        put_field(hc2t, k, DILATE_TWO, hg2[k, C:, :])
+
+    rows(BC + 16, place2t)
 
     def outer2(k):
         base = halo_z.own[k].astype(F32)
@@ -712,7 +792,8 @@
         dec[k] = ((one.astype(F32) + two.astype(F32)) * 0.5).astype(BF)
 
     rows(BC, outer2, 16)
-    dec_copy = pltpu.make_async_copy(dec, dec_out, out_sem.at[1])
+    by_channel(dec, dec_nat)
+    dec_copy = pltpu.make_async_copy(dec_nat, dec_out, out_sem.at[1])
     dec_copy.start()
     early.start3()
     late.start3()
@@ -732,30 +813,25 @@
         copy.wait()
 
 
-def finish_kernel(dec_in, g0_in, early_in, late_in, out_dec, out_g0, out_a1, out_b1, out_a2, out_b2, *rest):
-    held, sems = rest[:4], rest[4]
-    loads = [
+def finish_kernel(dec_in, g0_in, early_in, late_in, out_dec, out_g0, out_a1, out_b1, out_a2, out_b2, early, late, sems):
+    copies = [
         pltpu.make_async_copy(src, dst, sems.at[k])
-        for k, (src, dst) in enumerate(zip((dec_in, g0_in, early_in, late_in), held))
+        for k, (src, dst) in enumerate(
+            ((late_in, late), (early_in, early), (dec_in, out_dec), (g0_in, out_g0))
+        )
     ]
-    for load in loads:
-        load.start()
-    back = permutation(True)
-    for load, src, dst in zip(loads, held, (out_dec, out_g0)):
-        load.wait()
-        whole = src[...].astype(F32)
-        for t in range(4):
-            part = whole[:, 8 * t : 8 * t + 8, :].reshape(256, BR).astype(BF)
-            dst[8 * t : 8 * t + 8] = dot(back, part).astype(BF).reshape(8, BC, BR)
-    early, late = held[2:]
-    loads[2].wait()
-    loads[3].wait()
+    for copy in copies:
+        copy.start()
+    copies[0].wait()
+    copies[1].wait()
     owners = early.shape[0]
     for src, which, dst in ((late, 0, out_a1), (early, 0, out_b1), (early, 1, out_a2), (early, 2, out_b2)):
         band = src[:, which].reshape(3 * C, BR)
         for p in range(3):
             for q in range(3):
                 dst[p, q] = band[p * C : p * C + C, q * C : q * C + C]
+    copies[2].wait()
+    copies[3].wait()
 
 
 def per_device(nrow, ncol, *arrays):
@@ -796,14 +872,16 @@
             vmem((BC, C, BR), BF),
             vmem((BC + 16, C, BR), BF),
             vmem((BC + 32, C, BR), BF),
+            vmem((C, BC, BR), BF),
+            vmem((C, BC, BR), BF),
         ]
     )
     whole = pl.BlockSpec(memory_space=pltpu.VMEM)
     anywhere = pl.BlockSpec(memory_space=pl.ANY)
-    by_bin = jax.ShapeDtypeStruct((BC, C, BR), BF)
+    field = jax.ShapeDtypeStruct((C, BC, BR), BF)
     results = pl.pallas_call(
         functools.partial(main_kernel, nrow, ncol),
-        out_shape=[by_bin, by_bin] + [jax.ShapeDtypeStruct(shape, F32) for shape in grad_shapes],
+        out_shape=[field, field] + [jax.ShapeDtypeStruct(shape, F32) for shape in grad_shapes],
         in_specs=[anywhere] * 6,
         out_specs=[anywhere] * 4,
         scratch_shapes=scratch,
@@ -813,14 +891,12 @@
         name="blocks",
     )(*arrays)
     small = jax.ShapeDtypeStruct((3, 3, C, C), F32)
-    field = jax.ShapeDtypeStruct((C, BC, BR), BF)
     return pl.pallas_call(
         finish_kernel,
         out_shape=[field, field, small, small, small, small],
         in_specs=[anywhere] * 4,
         out_specs=[whole] * 6,
-        scratch_shapes=[vmem((BC, C, BR), BF)] * 2
-        + [vmem(shape, F32) for shape in grad_shapes]
+        scratch_shapes=[vmem(shape, F32) for shape in grad_shapes]
         + [pltpu.SemaphoreType.DMA((4,))],
         compiler_params=pltpu.CompilerParams(vmem_limit_bytes=56 << 20),
         name="finish",

time: 101 us -> 89.8 us (0.89)
  Pallas kernels: 99.8 us -> 89.1 us
    pallas_call x1, Pallas kernels: 97.3 us -> 86.9 us  [per_device(): pl.pallas_call(functools.partial(main_kernel, nrow, ncol), out_shape=[fie...]
where the time goes in v4:
time: 89.8 us; the launch traced here: 89.7 us
  Pallas kernels  89.1 us (99%)
    pallas_call x1, Pallas kernels, per_device(): pl.pallas_call(functools.partial(main_kernel, nrow, ncol), out_shape=[fie...  86.9 us
    pallas_call x1, Pallas kernels, per_device(): pl.pallas_call(finish_kernel, out_shape=[field, field, small, small, smal...  2.15 us

profile of v4, /device:TPU:1, one launch (start us, length us, event | category | flops | bytes accessed | tf_op | source)
XLA Modules:
  0.0 89.7 jit_solution(8021228905091308433)
XLA Ops:
  0.6 86.9 %blocks.1 = (bf16[32,32,128]{2,1,0:T(8,128)(2,1)}, bf16[32,32,128]{2,1,0:T(8,128)(2,1)}, f32[12,3,8,128]{3,2,1,0:T(8,128)}, f32[12,1,8,128]{3,2,1,0:T(8,128)}) custom-call(bf16[32,32,128]{2,1,0:T(8,128)(2,1)} %refs_0_.1, bf16[32,32,128]{2,1,0:T(8,128)(2,1)} %refs_1_.1, bf16[3,3,32,32]{3,2,1,0:T(8,128)(2,1)} %refs_2_.1, bf16[3,3,32,32]{3,2,1,0:T(8,128)(2,1)} %refs_3_.1, ...), custom_call_target="tpu_custom_call" | custom-call | tf_op jit(solution)/shard_map/blocks/pallas_call | solution.py:882
  87.6 2.1 %finish.1 = (bf16[32,32,128]{2,1,0:T(8,128)(2,1)}, bf16[32,32,128]{2,1,0:T(8,128)(2,1)}, f32[3,3,32,32]{3,2,1,0:T(8,128)}, f32[3,3,32,32]{3,2,1,0:T(8,128)}, f32...) custom-call(bf16[32,32,128]{2,1,0:T(8,128)(2,1)} %get-tuple-element.10.dec_in, ...), custom_call_target="tpu_custom_call" | custom-call | tf_op jit(solution)/shard_map/finish/pallas_call | solution.py:894

commit v5 on v4

--- a/solution.py
+++ b/solution.py
@@ -560,7 +560,7 @@
 
     place = Place(nrow, ncol)
     ri, ci = place.ri, place.ci
-    halo_x = Halo(8, place, take(7))
+    halo_x = Halo(8, place, take(7), True)
     halo_s2 = Halo(16, place, take(7), True)
     halo_z = Halo(16, place, take(7), True)
     halo_s1 = Halo(8, place, take(7))
@@ -649,9 +649,9 @@
 
     d = DILATE_ONE
     halo_x.prepare(xc1, d)
-    halo_x.wait()
+    halo_x.forward()
     mir_g.forward()
-    halo_x.build(xc1, d)
+    halo_x.build(xc1, d, outer=False)
 
     def hidden1(k):
         pre = dot(wa1[...], taps(xc1, k, d))
@@ -659,7 +659,16 @@
         slope1[k] = sig * (1.0 + pre * (1.0 - sig))
         put_field(hc1, k, d, pre * sig)
 
-    rows(BC + 2 * d, hidden1, 10)
+    rows(24, hidden1, 12, 8)
+    halo_x.wait()
+    halo_x.build(xc1, d, inner=False)
+
+    def edge1(t, carry):
+        for u in range(8):
+            hidden1(t * 32 + u)
+        return carry
+
+    lax.fori_loop(0, 2, edge1, 0)
 
     def outer1(k):
         y1[k] = (halo_x.own[k].astype(F32) + dot(wb1[...], taps(hc1, k, d))).astype(BF)
@@ -689,8 +698,6 @@
     halo_s2.pack_sides()
     halo_s2.start()
     halo_s2.prepare(sc2, DILATE_TWO)
-    halo_s2.forward()
-    halo_s2.build(sc2, DILATE_TWO, outer=False)
 
     mir_y.wait()
     turned = mir_y.fetch()
@@ -703,6 +710,8 @@
     halo_z.own[...] = ((y1[...].astype(F32) + interleave(parts)) * 0.5).astype(BF)
     halo_z.pack_sides()
     halo_z.start()
+    halo_s2.forward()
+    halo_s2.build(sc2, DILATE_TWO, outer=False)
     halo_z.prepare(xc2, DILATE_TWO)
 
     d = DILATE_TWO

time: 89.8 us -> 87.7 us (0.977)
  Pallas kernels: 89.1 us -> 87 us
    pallas_call x1, Pallas kernels: 86.9 us -> 84.8 us  [per_device(): pl.pallas_call(functools.partial(main_kernel, nrow, ncol), out_shape=[fie...]
where the time goes in v5:
time: 87.7 us; the launch traced here: 87.6 us
  Pallas kernels  87 us (99%)
    pallas_call x1, Pallas kernels, per_device(): pl.pallas_call(functools.partial(main_kernel, nrow, ncol), out_shape=[fie...  84.8 us
    pallas_call x1, Pallas kernels, per_device(): pl.pallas_call(finish_kernel, out_shape=[field, field, small, small, smal...  2.15 us

profile of v5, /device:TPU:1, one launch (start us, length us, event | category | flops | bytes accessed | tf_op | source)
XLA Modules:
  0.0 87.6 jit_solution(2088853699627324963)
XLA Ops:
  0.6 84.8 %blocks.1 = (bf16[32,32,128]{2,1,0:T(8,128)(2,1)}, bf16[32,32,128]{2,1,0:T(8,128)(2,1)}, f32[12,3,8,128]{3,2,1,0:T(8,128)}, f32[12,1,8,128]{3,2,1,0:T(8,128)}) custom-call(bf16[32,32,128]{2,1,0:T(8,128)(2,1)} %refs_0_.1, bf16[32,32,128]{2,1,0:T(8,128)(2,1)} %refs_1_.1, bf16[3,3,32,32]{3,2,1,0:T(8,128)(2,1)} %refs_2_.1, bf16[3,3,32,32]{3,2,1,0:T(8,128)(2,1)} %refs_3_.1, ...), custom_call_target="tpu_custom_call" | custom-call | tf_op jit(solution)/shard_map/blocks/pallas_call | solution.py:891
  85.5 2.1 %finish.1 = (bf16[32,32,128]{2,1,0:T(8,128)(2,1)}, bf16[32,32,128]{2,1,0:T(8,128)(2,1)}, f32[3,3,32,32]{3,2,1,0:T(8,128)}, f32[3,3,32,32]{3,2,1,0:T(8,128)}, f32...) custom-call(bf16[32,32,128]{2,1,0:T(8,128)(2,1)} %get-tuple-element.10.dec_in, ...), custom_call_target="tpu_custom_call" | custom-call | tf_op jit(solution)/shard_map/finish/pallas_call | solution.py:903

commit v6 on v5

--- a/solution.py
+++ b/solution.py
@@ -659,7 +659,7 @@
         slope1[k] = sig * (1.0 + pre * (1.0 - sig))
         put_field(hc1, k, d, pre * sig)
 
-    rows(24, hidden1, 12, 8)
+    rows(24, hidden1, 24, 8)
     halo_x.wait()
     halo_x.build(xc1, d, inner=False)
 
@@ -734,10 +734,10 @@
         put_field(ec2, k, d, grad[:C])
         put_field(ec2t, k, d, grad[C:])
 
-    rows(16, hidden2, 8, 16)
+    rows(16, hidden2, 16, 16)
     halo_z.wait()
     halo_z.build(xc2, d, inner=False)
-    outer_rows(hidden2, 8)
+    outer_rows(hidden2, 16)
 
     def upstream1(k):
         base = halo_s2.own[k].astype(F32)
@@ -768,7 +768,7 @@
     def cotangent1(k):
         put_field(ec1, k, d, dot(tb1[...], taps(sc1, k, d)) * slope1[k])
 
-    rows(BC + 2 * d, cotangent1, 10)
+    rows(BC + 2 * d, cotangent1, 20)
     kernel_grad(
         pad1, lambda k: ec1[k + DILATE_ONE, C : 2 * C, :], xc1.at[d : d + BC + 2 * d], d, late.acc, 0
     )

time: 87.7 us -> 87.7 us (level)
  no operation moved by 1% of the time
where the time goes in v6:
time: 87.7 us; the launch traced here: 87.6 us
  Pallas kernels  87 us (99%)
    pallas_call x1, Pallas kernels, per_device(): pl.pallas_call(functools.partial(main_kernel, nrow, ncol), out_shape=[fie...  84.8 us
    pallas_call x1, Pallas kernels, per_device(): pl.pallas_call(finish_kernel, out_shape=[field, field, small, small, smal...  2.15 us

profile of v6, /device:TPU:1, one launch (start us, length us, event | category | flops | bytes accessed | tf_op | source)
XLA Modules:
  0.0 87.6 jit_solution(3267141558028267713)
XLA Ops:
  0.6 84.8 %blocks.1 = (bf16[32,32,128]{2,1,0:T(8,128)(2,1)}, bf16[32,32,128]{2,1,0:T(8,128)(2,1)}, f32[12,3,8,128]{3,2,1,0:T(8,128)}, f32[12,1,8,128]{3,2,1,0:T(8,128)}) custom-call(bf16[32,32,128]{2,1,0:T(8,128)(2,1)} %refs_0_.1, bf16[32,32,128]{2,1,0:T(8,128)(2,1)} %refs_1_.1, bf16[3,3,32,32]{3,2,1,0:T(8,128)(2,1)} %refs_2_.1, bf16[3,3,32,32]{3,2,1,0:T(8,128)(2,1)} %refs_3_.1, ...), custom_call_target="tpu_custom_call" | custom-call | tf_op jit(solution)/shard_map/blocks/pallas_call | solution.py:891
  85.5 2.1 %finish.1 = (bf16[32,32,128]{2,1,0:T(8,128)(2,1)}, bf16[32,32,128]{2,1,0:T(8,128)(2,1)}, f32[3,3,32,32]{3,2,1,0:T(8,128)}, f32[3,3,32,32]{3,2,1,0:T(8,128)}, f32...) custom-call(bf16[32,32,128]{2,1,0:T(8,128)(2,1)} %get-tuple-element.10.dec_in, ...), custom_call_target="tpu_custom_call" | custom-call | tf_op jit(solution)/shard_map/finish/pallas_call | solution.py:903
